TPU v7x, 32 devices: a whole 2x2x4 slice. The times are simulated.
32 devices in a mesh: dp: 8 (over z, y), tensor: 4 (over x, core).
Axes of the slice: x: 2, y: 2, z: 4, core: 2. Of those that a mesh axis runs over, the one named last changes fastest.
Arguments:
- tokens: bfloat16 [8192, 1024], P('dp'), may hold values from -6 to 6
- positions: int32 [8192], P('dp'), may hold values from 0 to 1023, as said below
- routes: int32 [8192, 8], P('dp'), may hold values from 0 to 31, all different within a row; in each aligned block of 1024 rows (0 to 1023, 1024 to 2047, ...) at most 384 rows name the same one
- gates: float32 [8192, 8], P('dp'), may hold values from 0.06 to 0.19
- norm1_gain: float32 [1024], replicated, may hold values from 0.5 to 1.5
- w_query: bfloat16 [1024, 1024], P(None, 'tensor'), may hold values from -0.25 to 0.25
- w_key: bfloat16 [1024, 512], P(None, 'tensor'), may hold values from -0.25 to 0.25
- w_value: bfloat16 [1024, 512], P(None, 'tensor'), may hold values from -0.1875 to 0.1875
- w_out: bfloat16 [1024, 1024], P('tensor'), may hold values from -0.75 to 0.75
- norm2_gain: float32 [1024], replicated, may hold values from 0.5 to 1.5
- w_gate: bfloat16 [32, 1024, 512], P(None, None, 'tensor'), may hold values from -0.1875 to 0.1875
- w_up: bfloat16 [32, 1024, 512], P(None, None, 'tensor'), may hold values from -0.1875 to 0.1875
- w_down: bfloat16 [32, 512, 1024], P(None, 'tensor'), may hold values from -0.75 to 0.75
- out_grad: bfloat16 [8192, 1024], P('dp'), may hold values from -6 to 6
Outputs:
- block_out: float32 [8192, 1024], P('dp')
- tokens_grad: float32 [8192, 1024], P('dp')
- grad_norm1_gain: float32 [1024], P('dp')
- grad_w_query: float32 [1024, 1024], P('dp', 'tensor')
- grad_w_key: float32 [1024, 512], P('dp', 'tensor')
- grad_w_value: float32 [1024, 512], P('dp', 'tensor')
- grad_w_out: float32 [1024, 1024], P('tensor', 'dp')
- grad_norm2_gain: float32 [1024], P('dp')
- grad_w_gate: float32 [32, 1024, 512], P(None, 'dp', 'tensor')
- grad_w_up: float32 [32, 1024, 512], P(None, 'dp', 'tensor')
- grad_w_down: float32 [32, 512, 1024], P(None, 'tensor', 'dp')
Inputs may be any that keep to these rules, and one draw needn't show every extreme that they name: Within each sequence of 1024 rows positions count up by one and start again at 0 where a new document begins; the first row of each sequence begins a document; in every draw some sequence is one whole document. `routes`: A token names 8 different experts; in the 1024 rows of one device no expert is named by more than 384 rows, and in every draw some expert is named by exactly 384 rows of some device.
All inputs are finite; a program needn't handle non-finite values.
Results may differ from a plain program's by a relative error of at most 0.014.
Values sent between devices are 32-bit elements; how exact they have to be, the bound alone decides.
No kernel may reach another device: no remote copies, remote signals or barrier semaphores. Data moves between devices by JAX's collectives and lax.ppermute only.
A program may use at most 384 MiB of HBM per device.

v0:
```python
import jax
import jax.numpy as jnp
from jax import lax
from jax.sharding import PartitionSpec as P

HEAD_DIM = 64
EXPERTS = 32
TOP = 8
CAP = 384


EPS = 1e-06
ROPE_BASE = 10000.0


def rms_norm(values_in, gain_in):
    return values_in * lax.rsqrt(jnp.mean(values_in * values_in, -1, keepdims=True) + EPS) * gain_in


def rope_tables(positions):
    half_dim = HEAD_DIM // 2
    freqs = ROPE_BASE ** (-(jnp.arange(half_dim, dtype=jnp.float32) * 2.0) / HEAD_DIM)
    angles = positions.astype(jnp.float32)[:, None] * freqs[None, :]
    cosine = jnp.cos(angles)
    sine_table = jnp.sin(angles)
    return (jnp.concatenate([cosine, cosine], -1), jnp.concatenate([sine_table, sine_table], -1))


def rotate(values_in, cosine, sine_table):
    half_dim = values_in.shape[-1] // 2
    turned = jnp.concatenate([-values_in[..., half_dim:], values_in[..., :half_dim]], -1)
    return values_in * cosine[:, None, :] + turned * sine_table[:, None, :]


def swiglu(gate_in, up_in):
    return jax.nn.silu(gate_in) * up_in


def per_device(
    tokens,
    positions,
    routes,
    gates,
    norm1_gain,
    w_query,
    w_key,
    w_value,
    w_out,
    norm2_gain,
    w_gate,
    w_up,
    w_down,
    out_grad,
):
    bfloat = jnp.bfloat16
    wide = jnp.float32
    row_count = tokens.shape[0]
    local_heads = w_query.shape[1] // HEAD_DIM
    local_groups = w_key.shape[1] // HEAD_DIM
    per_group = local_heads // local_groups
    scale_factor = HEAD_DIM ** (-0.5)
    block_rows = min(512, row_count)
    block_count = row_count // block_rows
    tokens_wide = tokens.astype(wide)
    normed1, norm1_back = jax.vjp(rms_norm, tokens_wide, norm1_gain)
    normed1_low = normed1.astype(bfloat)
    query_proj = jnp.dot(normed1_low, w_query, preferred_element_type=wide)
    key_proj = jnp.dot(normed1_low, w_key, preferred_element_type=wide)
    value_low = (
        jnp.dot(normed1_low, w_value, preferred_element_type=wide)
        .astype(bfloat)
        .reshape(row_count, local_groups, HEAD_DIM)
    )
    cosine, sine_table = rope_tables(positions)

    def turn_query(proj_in):
        return rotate(proj_in.reshape(row_count, local_heads, HEAD_DIM), cosine, sine_table)

    def turn_key(proj_in):
        return rotate(proj_in.reshape(row_count, local_groups, HEAD_DIM), cosine, sine_table)

    query_rot, query_back = jax.vjp(turn_query, query_proj)
    key_rot, key_back = jax.vjp(turn_key, key_proj)
    query_low = query_rot.astype(bfloat).reshape(row_count, local_groups, per_group, HEAD_DIM)
    key_low = key_rot.astype(bfloat)
    key_index = jnp.arange(row_count, dtype=jnp.int32)

    def block_scores(block_num):
        row_start = block_num * block_rows
        query_block = query_low[row_start : row_start + block_rows]
        row_index = row_start + jnp.arange(block_rows, dtype=jnp.int32)
        place_gap = positions[row_start : row_start + block_rows][:, None] - positions[None, :]
        allowed = (row_index[:, None] >= key_index[None, :]) & (
            place_gap == row_index[:, None] - key_index[None, :]
        )
        raw_scores = (
            jnp.einsum("qgrd,kgd->grqk", query_block, key_low, preferred_element_type=wide)
            * scale_factor
        )
        return (jnp.where(allowed[None, None], raw_scores, -1e30), query_block)

    mixed_blocks = []
    log_totals = []
    for block_num in range(block_count):
        scores, query_block = block_scores(block_num)
        row_max = jnp.max(scores, -1, keepdims=True)
        exp_scores = jnp.exp(scores - row_max)
        row_total = jnp.sum(exp_scores, -1, keepdims=True)
        soft_low = (exp_scores / row_total).astype(bfloat)
        log_totals.append(row_max + jnp.log(row_total))
        mixed_blocks.append(
            jnp.einsum("grqk,kgd->qgrd", soft_low, value_low, preferred_element_type=wide)
        )
    mixed_low = (
        jnp.concatenate(mixed_blocks, 0).astype(bfloat).reshape(row_count, local_heads * HEAD_DIM)
    )
    attn_part = jnp.dot(mixed_low, w_out, preferred_element_type=wide)
    attention = lax.psum(attn_part, "tensor")
    hidden = tokens_wide + attention
    normed2, norm2_back = jax.vjp(rms_norm, hidden, norm2_gain)
    normed2_low = normed2.astype(bfloat)
    chosen = routes.reshape(-1)
    onehot = (chosen[:, None] == jnp.arange(EXPERTS, dtype=jnp.int32)[None, :]).astype(jnp.int32)
    before = jnp.cumsum(onehot, 0) - onehot
    slot_rank = jnp.sum(before * onehot, 1)
    target = chosen * CAP + slot_rank
    source = jnp.arange(row_count * TOP, dtype=jnp.int32) // TOP
    slot_owner = jnp.zeros((EXPERTS * CAP,), jnp.int32).at[target].set(source)
    filled = jnp.zeros((EXPERTS * CAP,), bfloat).at[target].set(1.0)
    sent_rows = (normed2_low[slot_owner] * filled[:, None]).reshape(EXPERTS, CAP, -1)
    gate_part = jnp.einsum("ecd,edf->ecf", sent_rows, w_gate, preferred_element_type=wide)
    up_part = jnp.einsum("ecd,edf->ecf", sent_rows, w_up, preferred_element_type=wide)
    active, swiglu_back = jax.vjp(swiglu, gate_part, up_part)
    active_low = active.astype(bfloat)
    result = jnp.einsum("ecf,efd->ecd", active_low, w_down, preferred_element_type=wide).reshape(
        EXPERTS * CAP, -1
    )
    picked = result[target].reshape(row_count, TOP, -1)
    expert_part = jnp.sum(gates[..., None] * picked, 1)
    expert_total = lax.psum(expert_part, "tensor")
    block_out = hidden + expert_total
    out_wide = out_grad.astype(wide)
    slot_gate = jnp.zeros((EXPERTS * CAP,), wide).at[target].set(gates.reshape(-1))
    result_grad = (
        (out_wide[slot_owner] * slot_gate[:, None]).astype(bfloat).reshape(EXPERTS, CAP, -1)
    )
    grad_w_down = jnp.einsum("ecf,ecd->efd", active_low, result_grad, preferred_element_type=wide)
    active_grad = jnp.einsum("ecd,efd->ecf", result_grad, w_down, preferred_element_type=wide)
    gate_grad, up_grad = swiglu_back(active_grad)
    gate_grad_low = gate_grad.astype(bfloat)
    up_grad_low = up_grad.astype(bfloat)
    grad_w_gate = jnp.einsum("ecd,ecf->edf", sent_rows, gate_grad_low, preferred_element_type=wide)
    grad_w_up = jnp.einsum("ecd,ecf->edf", sent_rows, up_grad_low, preferred_element_type=wide)
    sent_grad = jnp.einsum("ecf,edf->ecd", gate_grad_low, w_gate, preferred_element_type=wide)
    sent_grad = sent_grad + jnp.einsum(
        "ecf,edf->ecd", up_grad_low, w_up, preferred_element_type=wide
    )
    normed2_part = jnp.sum(
        sent_grad.reshape(EXPERTS * CAP, -1)[target].reshape(row_count, TOP, -1), 1
    )
    normed2_grad = lax.psum(normed2_part, "tensor")
    hidden_part, gain2_grad = norm2_back(normed2_grad)
    hidden_grad = out_wide + hidden_part
    attn_grad = hidden_grad.astype(bfloat)
    grad_w_out = jnp.einsum("tc,td->cd", mixed_low, attn_grad, preferred_element_type=wide)
    mixed_grad = jnp.einsum("td,cd->tc", attn_grad, w_out, preferred_element_type=wide).astype(
        bfloat
    )
    mixed_grad = mixed_grad.reshape(row_count, local_groups, per_group, HEAD_DIM)
    key_grad = jnp.zeros((row_count, local_groups, HEAD_DIM), wide)
    value_grad = jnp.zeros((row_count, local_groups, HEAD_DIM), wide)
    query_grads = []
    for block_num in range(block_count):
        row_start = block_num * block_rows
        scores, query_block = block_scores(block_num)
        soft = jnp.exp(scores - log_totals[block_num])
        grad_block = mixed_grad[row_start : row_start + block_rows]
        prob_grad = jnp.einsum("qgrd,kgd->grqk", grad_block, value_low, preferred_element_type=wide)
        row_dot = jnp.sum(soft * prob_grad, -1, keepdims=True)
        score_grad = (soft * (prob_grad - row_dot)).astype(bfloat)
        query_grads.append(
            jnp.einsum("grqk,kgd->qgrd", score_grad, key_low, preferred_element_type=wide)
            * scale_factor
        )
        key_grad = (
            key_grad
            + jnp.einsum("grqk,qgrd->kgd", score_grad, query_block, preferred_element_type=wide)
            * scale_factor
        )
        value_grad = value_grad + jnp.einsum(
            "grqk,qgrd->kgd", soft.astype(bfloat), grad_block, preferred_element_type=wide
        )
    query_rot_grad = jnp.concatenate(query_grads, 0).reshape(row_count, local_heads, HEAD_DIM)
    (query_in,) = query_back(query_rot_grad)
    (key_in,) = key_back(key_grad)
    query_in_low = query_in.astype(bfloat)
    key_in_low = key_in.astype(bfloat)
    value_in_low = value_grad.astype(bfloat).reshape(row_count, local_groups * HEAD_DIM)
    grad_w_query = jnp.einsum("td,tc->dc", normed1_low, query_in_low, preferred_element_type=wide)
    grad_w_key = jnp.einsum("td,tc->dc", normed1_low, key_in_low, preferred_element_type=wide)
    grad_w_value = jnp.einsum("td,tc->dc", normed1_low, value_in_low, preferred_element_type=wide)
    normed1_part = jnp.einsum("tc,dc->td", query_in_low, w_query, preferred_element_type=wide)
    normed1_part = normed1_part + jnp.einsum(
        "tc,dc->td", key_in_low, w_key, preferred_element_type=wide
    )
    normed1_part = normed1_part + jnp.einsum(
        "tc,dc->td", value_in_low, w_value, preferred_element_type=wide
    )
    normed1_grad = lax.psum(normed1_part, "tensor")
    tokens_part, gain1_grad = norm1_back(normed1_grad)
    tokens_grad = hidden_grad + tokens_part
    summed = (
        lax.psum_scatter(gain1_grad, "dp", scatter_dimension=0, tiled=True),
        lax.psum_scatter(grad_w_query, "dp", scatter_dimension=0, tiled=True),
        lax.psum_scatter(grad_w_key, "dp", scatter_dimension=0, tiled=True),
        lax.psum_scatter(grad_w_value, "dp", scatter_dimension=0, tiled=True),
        lax.psum_scatter(grad_w_out, "dp", scatter_dimension=1, tiled=True),
        lax.psum_scatter(grad_w_gate, "dp", scatter_dimension=1, tiled=True),
        lax.psum_scatter(grad_w_up, "dp", scatter_dimension=1, tiled=True),
        lax.psum_scatter(grad_w_down, "dp", scatter_dimension=2, tiled=True),
        lax.psum_scatter(gain2_grad, "dp", scatter_dimension=0, tiled=True),
    )
    return (
        block_out,
        tokens_grad,
        summed[0],
        summed[1],
        summed[2],
        summed[3],
        summed[4],
        summed[8],
        summed[5],
        summed[6],
        summed[7],
    )


def solution(mesh):
    placed = (
        P("dp", None),
        P("dp"),
        P("dp", None),
        P("dp", None),
        P(),
        P(None, "tensor"),
        P(None, "tensor"),
        P(None, "tensor"),
        P("tensor", None),
        P(),
        P(None, None, "tensor"),
        P(None, None, "tensor"),
        P(None, "tensor", None),
        P("dp", None),
    )
    return jax.shard_map(
        per_device,
        mesh=mesh,
        in_specs=placed,
        out_specs=(
            P("dp", None),
            P("dp", None),
            P("dp"),
            P("dp", "tensor"),
            P("dp", "tensor"),
            P("dp", "tensor"),
            P("tensor", "dp"),
            P("dp"),
            P(None, "dp", "tensor"),
            P(None, "dp", "tensor"),
            P(None, "tensor", "dp"),
        ),
        check_vma=False,
    )
```

profile of v0, /device:TPU:0, one launch (start us, length us, event | category | flops | bytes accessed | tf_op | source)
XLA Modules:
  0.0 1961.4 jit_solution(2353570186988027508)
XLA Ops:
  50.2 56.6 %scatter_custom_fusion.1 = bf16[12288]{0:T(1024)(128)(2,1)S(1)} fusion(s32[8192]{0:T(1024)S(1)} %bitcast.206, bf16[8192]{0:T(1024)(128)(2,1)S(1)} %broadcast.255, bf16[]{:T(256)} %constant.64.clone.1), kind=kCustom, calls=%fused_computation.159 | custom fusion | bytes 24578 | tf_op jit(solution)/shard_map/scatter | solution.py:129
  107.4 30.5 %scatter_custom_fusion.2 = f32[12288]{0:T(1024)S(1)} fusion(s32[8192]{0:T(1024)S(1)} %bitcast.207, f32[8192]{0:T(1024)S(1)} %reshape.387, f32[]{:T(128)} %constant.22.clone.1), kind=kCustom, calls=%fused_computation.153 | custom fusion | bytes 49156 | tf_op jit(solution)/shard_map/scatter | solution.py:143
  138.5 42.7 %scatter_custom_fusion = s32[12288]{0:T(1024)S(1)} fusion(s32[8192]{0:T(1024)S(1)} %bitcast.208, s32[8192]{0:T(1024)S(1)} %add_select_fusion, s32[]{:T(128)} %constant.56.clone.1), kind=kCustom, calls=%fused_computation.155 | custom fusion | bytes 49156 | tf_op jit(solution)/shard_map/scatter | solution.py:128
  185.4 67.2 %gather_fusion.2 = f32[12288,1024]{1,0:T(8,128)} fusion(f32[1024,1024]{1,0:T(8,128)} %convert_element_type.100, s32[12288]{0:T(1024)S(1)} %fusion.81), kind=kCustom, calls=%fused_computation.2 | custom fusion | bytes 100712448 | tf_op jit(solution)/shard_map/gather | solution.py:145
  259.7 52.5 %gather_fusion = bf16[12288,1024]{1,0:T(8,128)(2,1)} fusion(bf16[1024,1024]{1,0:T(8,128)(2,1)S(1)} %multiply_convert_fusion.5, s32[12288]{0:T(1024)S(1)} %fusion.81), kind=kCustom, calls=%fused_computation | custom fusion | bytes 50380800 | tf_op jit(solution)/shard_map/gather | solution.py:130
  312.3 32.2 %copy.61 = bf16[32,384,1024]{1,2,0:T(8,128)(2,1)} copy(bf16[32,384,1024]{2,1,0:T(8,128)(2,1)} %bitcast.177) | data formatting | bytes 50331648 | tf_op jit(solution)/shard_map/gather | solution.py:130
  361.9 17.5 fusion.7
  379.4 28.2 %multiply_convert_fusion.3 = (bf16[32,384,128]{2,1,0:T(8,128)(2,1)}, bf16[32,384,128]{2,1,0:T(8,128)(2,1)}, bf16[32,384,128]{2,1,0:T(8,128)(2,1)}) fusion(f32[32,384,128]{2,1,0:T(8,128)} %fusion.7, f32[32,384,128]{2,1,0:T(8,128)} %fusion.5, bf16[32,128,1024]{2,1,0:T(8,128)(2,1)} %param.26, f32[32,384,1024]{2,1,0:T(8,128)} %bitcast.171, ...), kind=kOutput, calls=%fused_computation.59 | convolution fusion | flops 3271557120 | bytes 80789504 | tf_op jit(solution)/shard_map/ecd,efd->ecf/dot_general | solution.py:148
  407.6 22.1 %fusion.105 = f32[32,384,1024]{2,1,0:T(8,128)} fusion(bf16[32,384,128]{2,1,0:T(8,128)(2,1)} %get-tuple-element.22, bf16[32,1024,128]{2,1,0:T(8,128)(2,1)} %param.24), kind=kOutput, calls=%fused_computation.183 | convolution fusion | flops 3221225472 | bytes 61865984 | tf_op jit(solution)/shard_map/ecf,edf->ecd/dot_general | solution.py:154
  429.7 37.6 %convolution_add_fusion = f32[32,384,1024]{2,1,0:T(8,128)} fusion(f32[32,384,1024]{2,1,0:T(8,128)} %fusion.105, bf16[32,384,128]{2,1,0:T(8,128)(2,1)} %get-tuple-element.21, bf16[32,1024,128]{2,1,0:T(8,128)(2,1)} %param.25), kind=kOutput, calls=%fused_computation.19 | convolution fusion | flops 3233808384 | bytes 112197632 | tf_op jit(solution)/shard_map/ecf,edf->ecd/dot_general | solution.py:155
  467.4 58.9 %gather_fusion.3 = f32[8192,1024]{1,0:T(8,128)} fusion(f32[12288,1024]{1,0:T(8,128)} %bitcast.169, s32[8192]{0:T(1024)S(1)} %copy-done.40), kind=kCustom, calls=%fused_computation.3 | custom fusion | bytes 67141632 | tf_op jit(solution)/shard_map/gather | solution.py:159
  543.3 23.4 %fusion.104 = f32[32,384,1024]{2,1,0:T(8,128)} fusion(bf16[32,384,128]{2,1,0:T(8,128)(2,1)} %get-tuple-element.23, bf16[32,128,1024]{2,1,0:T(8,128)(2,1)} %param.26), kind=kOutput, calls=%fused_computation.182 | convolution fusion | flops 3221225472 | bytes 61865984 | tf_op jit(solution)/shard_map/ecf,efd->ecd/dot_general | solution.py:135
  566.7 59.2 %gather_fusion.1 = f32[8192,1024]{1,0:T(8,128)} fusion(f32[12288,1024]{1,0:T(8,128)} %bitcast.170, s32[8192]{0:T(1024)S(1)} %copy-done.40), kind=kCustom, calls=%fused_computation.1 | custom fusion | bytes 67141632 | tf_op jit(solution)/shard_map/gather | solution.py:138
  625.9 17.7 fusion
  689.1 25.2 %fusion.13 = f32[32,128,1024]{2,1,0:T(8,128)} fusion(bf16[32,384,128]{2,1,0:T(8,128)(2,1)} %get-tuple-element.23, f32[32,384,1024]{2,1,0:T(8,128)} %bitcast.172, f32[32,384]{1,0:T(8,128)S(1)} %copy-done.39), kind=kOutput, calls=%fused_computation.24 | convolution fusion | flops 3246391296 | bytes 70303744 | tf_op jit(solution)/shard_map/ecf,ecd->efd/dot_general | solution.py:147
  750.0 82.7 %all-reduce.16.cloned.1.call-done = (f32[1024,1024]{1,0:T(8,128)}, f32[1024,1024]{1,0:T(8,128)}) async-done(((f32[1024,1024]{1,0:T(8,128)}, f32[1024,1024]{1,0:T(8,128)}), (f32[1024,1024]{1,0:T(8,128)}, f32[1024,1024]{1,0:T(8,128)})) %all-reduce.16.cloned.1.call-update) | async-done | bytes 8388624 | tf_op jit(solution)/shard_map/psum | solution.py:140
  841.1 21.8 %all-reduce.6 = (f32[1024]{0:T(1024)S(1)}, f32[1024]{0:T(1024)S(1)}) all-reduce(f32[1024]{0:T(1024)S(1)} %get-tuple-element.13, f32[1024]{0:T(1024)S(1)} %get-tuple-element.11), channel_id=2, replica_groups=mesh['dp'=8,'tensor'=4] {'dp'}, use_global_device_ids=true, to_apply=%region_23.24.clone | all-reduce | flops 2048 | bytes 16384
  869.6 28.9 %reduce-scatter.12.cloned.1.call-done = f32[128,128]{1,0:T(8,128)} async-done(((f32[1024,128]{1,0:T(8,128)}), f32[128,128]{1,0:T(8,128)}) %reduce-scatter.12.cloned.1.call-update) | async-done | bytes 65552 | tf_op jit(solution)/shard_map/reduce_scatter | solution.py:216
  898.5 65.0 %reduce-scatter.10.cloned.1.call-done = f32[128,128]{1,0:T(8,128)} async-done(((f32[1024,128]{1,0:T(8,128)}), f32[128,128]{1,0:T(8,128)}) %reduce-scatter.10.cloned.1.call-update) | async-done | bytes 65552 | tf_op jit(solution)/shard_map/reduce_scatter | solution.py:215
  963.6 66.8 %reduce-scatter.14.cloned.1.call-done = f32[256,128]{1,0:T(8,128)} async-done(((f32[256,1024]{1,0:T(8,128)}), f32[256,128]{1,0:T(8,128)}) %reduce-scatter.14.cloned.1.call-update) | async-done | bytes 131088 | tf_op jit(solution)/shard_map/reduce_scatter | solution.py:217
  1030.3 66.8 %reduce-scatter.8.cloned.1.call-done = f32[128,256]{1,0:T(8,128)} async-done(((f32[1024,256]{1,0:T(8,128)}), f32[128,256]{1,0:T(8,128)}) %reduce-scatter.8.cloned.1.call-update) | async-done | bytes 131088 | tf_op jit(solution)/shard_map/reduce_scatter | solution.py:214
  1097.1 286.1 %reduce-scatter.20.cloned.1.call-done = f32[32,128,128]{2,1,0:T(8,128)} async-done(((f32[32,128,1024]{2,1,0:T(8,128)}), f32[32,128,128]{2,1,0:T(8,128)}) %reduce-scatter.20.cloned.1.call-update) | async-done | bytes 2097168 | tf_op jit(solution)/shard_map/reduce_scatter | solution.py:220
  1383.2 286.0 %reduce-scatter.16.cloned.1.call-done = f32[32,128,128]{2,1,0:T(8,128)} async-done(((f32[32,1024,128]{2,1,0:T(8,128)}), f32[32,128,128]{2,1,0:T(8,128)}) %reduce-scatter.16.cloned.1.call-update) | async-done | bytes 2097168 | tf_op jit(solution)/shard_map/reduce_scatter | solution.py:218
  1669.1 285.2 %reduce-scatter.18.cloned.1.call-done = f32[32,128,128]{2,1,0:T(8,128)} async-done(((f32[32,1024,128]{2,1,0:T(8,128)}), f32[32,128,128]{2,1,0:T(8,128)}) %reduce-scatter.18.cloned.1.call-update) | async-done | bytes 2097168 | tf_op jit(solution)/shard_map/reduce_scatter | solution.py:219
  (242 shorter events, 184.5 us)
Async XLA Ops:
  7.2 25.9 %copy-start = (bf16[256,1024]{1,0:T(8,128)(2,1)S(1)}, bf16[256,1024]{1,0:T(8,128)(2,1)}, u32[]{:S(2)}) copy-start(bf16[256,1024]{1,0:T(8,128)(2,1)} %param.22) | copy-start | bytes 1572868
  7.2 247.2 %all-reduce.12.cloned.1.call-start = ((), (), s32[]{:S(2)}) async-start(), calls=%async_computation.7 | async-start | bytes 8388608 | tf_op jit(solution)/shard_map/psum | solution.py:118
  14.5 14.0 copy-start.18
  35.8 607.8 %all-reduce.14.cloned.1.call-start = ((), (), s32[]{:S(2)}) async-start(), calls=%async_computation.8 | async-start | bytes 8388608 | tf_op jit(solution)/shard_map/psum | solution.py:161
  37.5 12.3 copy-start.56
  50.0 135.4 %copy-start.12 = (f32[1024,8]{1,0:T(8,128)}, f32[1024,8]{1,0:T(8,128)S(1)}, u32[]{:S(2)}) copy-start(f32[1024,8]{1,0:T(8,128)S(1)} %copy.57) | copy-start | bytes 98308
  185.4 69.1 %copy-start.8 = (bf16[1024,1024]{1,0:T(8,128)(2,1)S(1)}, bf16[1024,1024]{1,0:T(8,128)(2,1)}, u32[]{:S(2)}) copy-start(bf16[1024,1024]{1,0:T(8,128)(2,1)} %param.14) | copy-start | bytes 6291460
  312.2 32.2 %copy-start.57 = (bf16[32,384]{1,0:T(8,128)(2,1)S(1)}, bf16[32,384]{1,0:T(8,128)(2,1)}, u32[]{:S(2)}) copy-start(bf16[32,384]{1,0:T(8,128)(2,1)} %mul.349) | copy-start | bytes 73732
  361.9 17.5 copy-start.38
  429.7 37.6 %copy-start.40 = (s32[8192]{0:T(1024)S(1)}, s32[8192]{0:T(1024)}, u32[]{:S(2)}) copy-start(s32[8192]{0:T(1024)} %broadcast_clamp_fusion) | copy-start | bytes 98308
  543.2 289.4 %all-reduce.16.cloned.1.call-start = ((), (), s32[]{:S(2)}) async-start(), calls=%async_computation.16 | async-start | bytes 16777216 | tf_op jit(solution)/shard_map/psum | solution.py:140
  566.7 59.2 %copy-start.13 = (f32[1024,8]{1,0:T(8,128)S(1)}, f32[1024,8]{1,0:T(8,128)}, u32[]{:S(2)}) copy-start(f32[1024,8]{1,0:T(8,128)} %copy-done.12) | copy-start | bytes 98308
  625.9 17.7 copy-start.45
  625.9 17.7 copy-start.54
  625.9 22.4 %copy-start.11 = (bf16[1024,1024]{1,0:T(8,128)(2,1)S(1)}, bf16[1024,1024]{1,0:T(8,128)(2,1)}, u32[]{:S(2)}) copy-start(bf16[1024,1024]{1,0:T(8,128)(2,1)} %param.27) | copy-start | bytes 6291460
  643.6 10.6 slice-start.2
  677.0 221.5 %reduce-scatter.12.cloned.1.call-start = ((), (), s32[]{:S(2)}) async-start(), calls=%async_computation.11 | async-start | bytes 589824 | tf_op jit(solution)/shard_map/reduce_scatter | solution.py:216
  680.2 283.4 %reduce-scatter.10.cloned.1.call-start = ((), (), s32[]{:S(2)}) async-start(), calls=%async_computation.10 | async-start | bytes 589824 | tf_op jit(solution)/shard_map/reduce_scatter | solution.py:215
  682.7 347.6 %reduce-scatter.14.cloned.1.call-start = ((), (), s32[]{:S(2)}) async-start(), calls=%async_computation.12 | async-start | bytes 1179648 | tf_op jit(solution)/shard_map/reduce_scatter | solution.py:217
  687.2 409.9 %reduce-scatter.8.cloned.1.call-start = ((), (), s32[]{:S(2)}) async-start(), calls=%async_computation.9 | async-start | bytes 1179648 | tf_op jit(solution)/shard_map/reduce_scatter | solution.py:214
  689.1 694.1 %reduce-scatter.20.cloned.1.call-start = ((), (), s32[]{:S(2)}) async-start(), calls=%async_computation.15 | async-start | bytes 18874368 | tf_op jit(solution)/shard_map/reduce_scatter | solution.py:220
  714.4 954.7 %reduce-scatter.16.cloned.1.call-start = ((), (), s32[]{:S(2)}) async-start(), calls=%async_computation.13 | async-start | bytes 18874368 | tf_op jit(solution)/shard_map/reduce_scatter | solution.py:218
  732.0 1222.3 %reduce-scatter.18.cloned.1.call-start = ((), (), s32[]{:S(2)}) async-start(), calls=%async_computation.14 | async-start | bytes 18874368 | tf_op jit(solution)/shard_map/reduce_scatter | solution.py:219
  839.6 24.5 %copy-start.49 = (f32[1024]{0:T(1024)S(1)}, f32[1024]{0:T(1024)}, u32[]{:S(2)}) copy-start(f32[1024]{0:T(1024)} %copy-done.48) | copy-start | bytes 12292
  (50 other events, 148.9 us)
Sparse Core Ops, SparseCore 0:
  35.9 88.1 all-reduce.11
  543.3 88.1 all-reduce.13
  677.1 155.4 all-reduce.15
  836.4 62.0 reduce-scatter.11
  902.7 60.8 reduce-scatter.9
  967.4 62.8 reduce-scatter.13
  1034.7 62.3 reduce-scatter.7
  1101.4 281.6 reduce-scatter.19
  1388.0 281.0 reduce-scatter.15
  1673.3 280.9 reduce-scatter.17
where the time goes:
time: 1970 us; the launch traced here: 1960 us
  waiting for transfers between devices  1170 us (59%)
  local copies, waits for them, and re-layouts  420 us (21%)
  matrix products  243 us (12%)
  other arithmetic  93.1 us (5%)
  blocking collectives  21.8 us (1%)
    reduce_scatter x1, waiting for transfers between devices, per_device(): lax.psum_scatter(grad_w_down, 'dp', scatter_dimension=2, tiled=True)  286 us
    reduce_scatter x1, waiting for transfers between devices, per_device(): lax.psum_scatter(grad_w_gate, 'dp', scatter_dimension=1, tiled=True)  286 us
    reduce_scatter x1, waiting for transfers between devices, per_device(): lax.psum_scatter(grad_w_up, 'dp', scatter_dimension=1, tiled=True)  285 us
    gather x2, local copies, waits for them, and re-layouts, per_device(): normed2_low[slot_owner] * filled[:, None]  84.7 us
    psum x1, waiting for transfers between devices, per_device(): expert_total = lax.psum(expert_part, 'tensor')  82.7 us
    gather x1, local copies, waits for them, and re-layouts, per_device(): out_wide[slot_owner] * slot_gate[:, None]  67.2 us
    reduce_scatter x1, waiting for transfers between devices, per_device(): lax.psum_scatter(grad_w_query, 'dp', scatter_dimension=0, tiled=True)  66.8 us
    reduce_scatter x1, waiting for transfers between devices, per_device(): lax.psum_scatter(grad_w_out, 'dp', scatter_dimension=1, tiled=True)  66.8 us
  transfers between devices with their start and end apart: 10, of which 8 were waited for; matrix products, arithmetic and copies ran while one was open for 20% of the time, Pallas kernels for 0%

commit v1 on v0

v1 whole, which is shorter than its diff:
```python
import functools

import jax
import jax.numpy as jnp
from jax import lax
from jax.experimental import pallas as pl
from jax.experimental.pallas import tpu as pltpu
from jax.sharding import PartitionSpec as P

HEAD_DIM = 64
EXPERTS = 32
TOP = 8
EPS = 1e-06
ROPE_BASE = 10000.0
CHUNKS = 4
ROWS = 512

bfloat = jnp.bfloat16
wide = jnp.float32

CORE_PAIRS = [(i, i ^ 1) for i in range(4)]
X_PAIRS = [(i, i ^ 2) for i in range(4)]


def dot_nn(a, b):
    return jnp.dot(a, b, preferred_element_type=wide)


def dot_nt(a, b):
    return lax.dot_general(a, b, (((1,), (1,)), ((), ())), preferred_element_type=wide)


def norm_forward(v, gain):
    return v * lax.rsqrt(jnp.mean(v * v, -1, keepdims=True) + EPS) * gain


def norm_backward(v, gain, q):
    r = lax.rsqrt(jnp.mean(v * v, -1, keepdims=True) + EPS)
    gq = gain * q
    v_grad = r * gq - v * (r * r * r) * jnp.mean(v * gq, -1, keepdims=True)
    return v_grad, jnp.sum(q * v * r, 0)


def rope_tables(positions):
    half_dim = HEAD_DIM // 2
    freqs = ROPE_BASE ** (-(jnp.arange(half_dim, dtype=jnp.float32) * 2.0) / HEAD_DIM)
    angles = positions.astype(jnp.float32)[:, None] * freqs[None, :]
    cosine = jnp.cos(angles)
    sine_table = jnp.sin(angles)
    return (jnp.concatenate([cosine, cosine], -1), jnp.concatenate([sine_table, sine_table], -1))


def rotate(values_in, cosine, sine_table):
    half_dim = values_in.shape[-1] // 2
    turned = jnp.concatenate([-values_in[..., half_dim:], values_in[..., :half_dim]], -1)
    return values_in * cosine[:, None, :] + turned * sine_table[:, None, :]


def expert_parts(x, og, gate_cols, w_pair, wd2):
    hidden = wd2.shape[0] // 2
    back = dot_nt(og, wd2)
    out = []
    for j in range(2):
        both = dot_nn(x, w_pair[j])
        gate, up = both[:, :hidden], both[:, hidden:]
        col = gate_cols[j]
        sig = 0.5 * jnp.tanh(0.5 * gate) + 0.5
        act = gate * sig
        slope = sig + act * (1.0 - sig)
        weighted = back[:, j * hidden : (j + 1) * hidden] * col
        out.append(
            (
                (act * up * col).astype(bfloat),
                (weighted * up * slope).astype(bfloat),
                (weighted * act).astype(bfloat),
            )
        )
    return out


def gate_columns(g, first):
    lane = lax.broadcasted_iota(jnp.int32, g.shape, 1)
    return [
        jnp.sum(jnp.where(lane == first + j, g, 0.0), axis=1, keepdims=True) for j in range(2)
    ]


def own_body(x_ref, og_ref, g_ref, wg_ref, wu_ref, wd_ref, ga_ref, gg_ref, ug_ref, n_ref):
    pair = pl.program_id(0)
    hidden = wg_ref.shape[2]

    @pl.when(pair == 0)
    def _():
        n_ref[...] = jnp.zeros_like(n_ref)

    w_pair = [jnp.concatenate([wg_ref[j], wu_ref[j]], axis=1) for j in range(2)]
    wd2 = wd_ref[...].reshape(2 * hidden, wd_ref.shape[2])
    cols = gate_columns(g_ref[...], 2 * pair)
    parts = expert_parts(x_ref[...], og_ref[...], cols, w_pair, wd2)
    total = n_ref[...]
    for j in range(2):
        ga, gg, ug = parts[j]
        lanes = slice(j * hidden, (j + 1) * hidden)
        ga_ref[:, lanes] = ga
        gg_ref[:, lanes] = gg
        ug_ref[:, lanes] = ug
        total = total + dot_nt(jnp.concatenate([gg, ug], axis=1), w_pair[j])
    n_ref[...] = total


def own_experts(x, og, g, w_gate, w_up, w_down):
    rows, width = x.shape
    experts, _, hidden = w_gate.shape
    full = lambda shape: pl.BlockSpec(shape, lambda p: (0, 0), pipeline_mode=pl.Buffered(1))
    act_shape = jax.ShapeDtypeStruct((rows, experts * hidden), bfloat)
    act_spec = pl.BlockSpec((rows, 2 * hidden), lambda p: (0, p))
    up_spec = pl.BlockSpec((2, width, hidden), lambda p: (p, 0, 0))
    return pl.pallas_call(
        own_body,
        grid=(experts // 2,),
        in_specs=[
            full((rows, width)),
            full((rows, width)),
            full((rows, experts)),
            up_spec,
            up_spec,
            pl.BlockSpec((2, hidden, width), lambda p: (p, 0, 0)),
        ],
        out_specs=[act_spec, act_spec, act_spec, pl.BlockSpec((rows, width), lambda p: (0, 0))],
        out_shape=[act_shape, act_shape, act_shape, jax.ShapeDtypeStruct((rows, width), wide)],
        compiler_params=pltpu.CompilerParams(
            dimension_semantics=("arbitrary",), vmem_limit_bytes=48 * 2**20
        ),
        cost_estimate=pl.CostEstimate(
            flops=10 * rows * width * experts * hidden,
            bytes_accessed=6 * experts * width * hidden + 6 * rows * experts * hidden,
            transcendentals=rows * experts * hidden,
        ),
        name="own_experts",
    )(x, og, g, w_gate, w_up, w_down)


def grads_body(
    first, other_rows,
    x_ref, og_ref, g_ref, xt_ref, ogt_ref,
    ga0_ref, gg0_ref, ug0_ref, ga1_ref, gg1_ref, ug1_ref,
    wg_ref, wu_ref, wd_ref,
    keep_g, send_g, keep_u, send_u, keep_d, send_d,
    s0_ref, s1_ref, sa_ref,
):
    pair = pl.program_id(0)
    hidden = wg_ref.shape[2]
    w_pair = [jnp.concatenate([wg_ref[j], wu_ref[j]], axis=1) for j in range(2)]
    wd2 = wd_ref[...].reshape(2 * hidden, wd_ref.shape[2])
    s_refs = (s0_ref, s1_ref)

    def block(i, _):
        rows = pl.ds(pl.multiple_of(i * ROWS, ROWS), ROWS)
        cols = gate_columns(g_ref[rows, :], 2 * (pair + first))
        parts = expert_parts(x_ref[rows, :], og_ref[rows, :], cols, w_pair, wd2)
        for j in range(2):
            ga, gg, ug = parts[j]
            lanes = slice(j * hidden, (j + 1) * hidden)
            sa_ref[rows, lanes] = ga
            s_refs[j][rows, :hidden] = gg
            s_refs[j][rows, hidden:] = ug
        return 0

    lax.fori_loop(0, other_rows // ROWS, block, 0)
    half = ga0_ref.shape[0]
    for own, (ga_ref, gg_ref, ug_ref) in enumerate(
        ((ga0_ref, gg0_ref, ug0_ref), (ga1_ref, gg1_ref, ug1_ref))
    ):
        rows = slice(other_rows + own * half, other_rows + (own + 1) * half)
        sa_ref[rows, :] = ga_ref[...]
        for j in range(2):
            lanes = slice(j * hidden, (j + 1) * hidden)
            s_refs[j][rows, :hidden] = gg_ref[:, lanes]
            s_refs[j][rows, hidden:] = ug_ref[:, lanes]
    shard = xt_ref.shape[0] // 2
    for j in range(2):
        grad = dot_nn(xt_ref[...], s_refs[j][...])
        keep_g[j] = grad[:shard, :hidden]
        send_g[j] = grad[shard:, :hidden]
        keep_u[j] = grad[:shard, hidden:]
        send_u[j] = grad[shard:, hidden:]
    down = dot_nn(ogt_ref[...], sa_ref[...])
    for j in range(2):
        turned = down[:, j * hidden : (j + 1) * hidden].T
        keep_d[j] = turned[:, :shard]
        send_d[j] = turned[:, shard:]


def expert_grads(chunk, x, og, g, xt, ogt, own0, own1, w_gate, w_up, w_down):
    other_rows, width = x.shape
    experts, _, hidden = w_gate.shape
    half = own0[0].shape[0]
    total_rows = other_rows + 2 * half
    shard = xt.shape[0] // 2
    count = experts // CHUNKS
    first = chunk * count // 2
    full = lambda a: pl.BlockSpec(a.shape, lambda p: (0, 0), pipeline_mode=pl.Buffered(1))
    own_spec = pl.BlockSpec((half, 2 * hidden), lambda p: (0, p + first))
    up_spec = pl.BlockSpec((2, width, hidden), lambda p: (p + first, 0, 0))
    out_spec = pl.BlockSpec((2, shard, hidden), lambda p: (p, 0, 0))
    down_spec = pl.BlockSpec((2, hidden, shard), lambda p: (p, 0, 0))
    up_shape = jax.ShapeDtypeStruct((count, shard, hidden), wide)
    down_shape = jax.ShapeDtypeStruct((count, hidden, shard), wide)
    return pl.pallas_call(
        functools.partial(grads_body, first, other_rows),
        grid=(count // 2,),
        in_specs=[full(x), full(og), full(g), full(xt), full(ogt)]
        + [own_spec] * 6
        + [up_spec, up_spec, pl.BlockSpec((2, hidden, width), lambda p: (p + first, 0, 0))],
        out_specs=[out_spec] * 4 + [down_spec] * 2,
        out_shape=[up_shape] * 4 + [down_shape] * 2,
        scratch_shapes=[pltpu.VMEM((total_rows, 2 * hidden), bfloat)] * 3,
        compiler_params=pltpu.CompilerParams(
            dimension_semantics=("arbitrary",), vmem_limit_bytes=56 * 2**20
        ),
        cost_estimate=pl.CostEstimate(
            flops=6 * other_rows * width * count * hidden + 12 * total_rows * shard * count * hidden,
            bytes_accessed=4 * other_rows * width + 6 * count * width * hidden,
            transcendentals=other_rows * count * hidden,
        ),
        name="expert_grads",
    )(x, og, g, xt, ogt, *own0, *own1, w_gate, w_up, w_down)


def per_device(
    dp_size,
    tokens,
    positions,
    routes,
    gates,
    norm1_gain,
    w_query,
    w_key,
    w_value,
    w_out,
    norm2_gain,
    w_gate,
    w_up,
    w_down,
    out_grad,
):
    row_count, width = tokens.shape
    half = row_count // 2
    local_heads = w_query.shape[1] // HEAD_DIM
    local_groups = w_key.shape[1] // HEAD_DIM
    per_group = local_heads // local_groups
    scale_factor = HEAD_DIM ** (-0.5)
    block_rows = min(512, row_count)
    block_count = row_count // block_rows
    core = lax.axis_index("tensor") % 2
    x_side = lax.axis_index("tensor") // 2
    dp_place = lax.axis_index("dp")
    small = dp_size == 8
    up_steps = [[(2 * z + y, 2 * z + 2 + y) for z in range(k - 1, 3) for y in range(2)] for k in (1, 2, 3)]
    down_steps = [[(2 * z + y, 2 * z - 2 + y) for z in range(1, 5 - k) for y in range(2)] for k in (1, 2, 3)]
    y_pairs = [(i, i ^ 1) for i in range(dp_size)]

    one = jnp.where(dp_place < 0, 0.5, 1.0).astype(wide)

    def rounded(v):
        return (v * one).astype(bfloat)

    def swap_core(v):
        return lax.ppermute(v, "tensor", CORE_PAIRS)

    def swap_x(v):
        return lax.ppermute(v, "tensor", X_PAIRS)

    def my_half(v):
        return lax.dynamic_slice_in_dim(v, core * half, half, 0)

    def other_half(v):
        return lax.dynamic_slice_in_dim(v, (1 - core) * half, half, 0)

    def natural(mine, other):
        return jnp.where(
            core == 0, jnp.concatenate([mine, other], 0), jnp.concatenate([other, mine], 0)
        )

    def total_half(mine, other):
        both = mine + swap_core(other)
        return both + swap_x(both)

    def along_z(v):
        z = dp_place // 2
        ups, downs = [v], [v]
        for k in range(3):
            ups.append(lax.ppermute(ups[-1], "dp", up_steps[k]))
            downs.append(lax.ppermute(downs[-1], "dp", down_steps[k]))
        return [jnp.where(z >= k, ups[k], downs[4 - k]) for k in (1, 2, 3)]

    def sum_blocks(blocks):
        if not small:
            return lax.psum_scatter(blocks, "dp", scatter_dimension=0, tiled=True)[0]
        y, z = dp_place % 2, dp_place // 2
        split = blocks.reshape((4, 2) + blocks.shape[1:])
        kept = lax.dynamic_index_in_dim(split, y, 1, False)
        sent = lax.dynamic_index_in_dim(split, 1 - y, 1, False)
        kept = kept + lax.ppermute(sent, "dp", y_pairs)
        total = lax.dynamic_index_in_dim(kept, z, 0, False)
        for k in (1, 2, 3):
            part = lax.dynamic_index_in_dim(kept, (z + k) % 4, 0, False)
            total = total + lax.ppermute(part, "dp", [(i, (i + 2 * k) % 8) for i in range(8)])
        return total

    out_wide = out_grad.astype(wide)
    lane = jnp.arange(EXPERTS, dtype=jnp.int32)
    dense_gates = jnp.sum(
        jnp.where(routes[:, :, None] == lane[None, None, :], gates[:, :, None], 0.0), 1
    )
    local_order = lambda v: jnp.concatenate([my_half(v), other_half(v)], 0)
    if small:
        og_z = along_z(my_half(out_wide))
        gates_z = along_z(dense_gates.T)

    tokens_wide = tokens.astype(wide)
    normed1_low = norm_forward(tokens_wide, norm1_gain).astype(bfloat)
    query_proj = dot_nn(normed1_low, w_query)
    key_proj = dot_nn(normed1_low, w_key)
    value_low = (
        dot_nn(normed1_low, w_value).astype(bfloat).reshape(row_count, local_groups, HEAD_DIM)
    )
    cosine, sine_table = rope_tables(positions)

    def turn_query(proj_in):
        return rotate(proj_in.reshape(row_count, local_heads, HEAD_DIM), cosine, sine_table)

    def turn_key(proj_in):
        return rotate(proj_in.reshape(row_count, local_groups, HEAD_DIM), cosine, sine_table)

    query_rot, query_back = jax.vjp(turn_query, query_proj)
    key_rot, key_back = jax.vjp(turn_key, key_proj)
    query_low = query_rot.astype(bfloat).reshape(row_count, local_groups, per_group, HEAD_DIM)
    key_low = key_rot.astype(bfloat)
    key_index = jnp.arange(row_count, dtype=jnp.int32)

    def block_scores(block_num):
        row_start = block_num * block_rows
        query_block = query_low[row_start : row_start + block_rows]
        row_index = row_start + jnp.arange(block_rows, dtype=jnp.int32)
        place_gap = positions[row_start : row_start + block_rows][:, None] - positions[None, :]
        allowed = (row_index[:, None] >= key_index[None, :]) & (
            place_gap == row_index[:, None] - key_index[None, :]
        )
        raw_scores = (
            jnp.einsum("qgrd,kgd->grqk", query_block, key_low, preferred_element_type=wide)
            * scale_factor
        )
        return (jnp.where(allowed[None, None], raw_scores, -1e30), query_block)

    mixed_blocks = []
    log_totals = []
    for block_num in range(block_count):
        scores, query_block = block_scores(block_num)
        row_max = jnp.max(scores, -1, keepdims=True)
        exp_scores = jnp.exp(scores - row_max)
        row_total = jnp.sum(exp_scores, -1, keepdims=True)
        soft_low = (exp_scores / row_total).astype(bfloat)
        log_totals.append(row_max + jnp.log(row_total))
        mixed_blocks.append(
            jnp.einsum("grqk,kgd->qgrd", soft_low, value_low, preferred_element_type=wide)
        )
    mixed_low = (
        jnp.concatenate(mixed_blocks, 0).astype(bfloat).reshape(row_count, local_heads * HEAD_DIM)
    )
    attention = total_half(
        dot_nn(my_half(mixed_low), w_out), dot_nn(other_half(mixed_low), w_out)
    )
    hidden = my_half(tokens_wide) + attention
    normed2 = norm_forward(hidden, norm2_gain)
    normed2_mine = normed2.astype(bfloat)
    normed2_other = rounded(swap_core(normed2))
    og_mine, og_other = my_half(out_grad), other_half(out_grad)
    gates_mine, gates_other = my_half(dense_gates), other_half(dense_gates)
    own_other = own_experts(normed2_other, og_other, gates_other, w_gate, w_up, w_down)
    own_mine = own_experts(normed2_mine, og_mine, gates_mine, w_gate, w_up, w_down)

    normed2_grad = total_half(own_mine[3], own_other[3])
    hidden_part, gain2_grad = norm_backward(hidden, norm2_gain, normed2_grad)
    hidden_grad = my_half(out_wide) + hidden_part
    attn_grad = natural(hidden_grad.astype(bfloat), rounded(swap_core(hidden_grad)))

    w_down2 = w_down.reshape(-1, width)
    expert_total = total_half(dot_nn(own_mine[0], w_down2), dot_nn(own_other[0], w_down2))
    block_mine = hidden + expert_total
    block_out = natural(block_mine, swap_core(block_mine))

    if small:
        quarter = half // 2
        normed2_z = along_z(lax.dynamic_slice_in_dim(normed2, x_side * quarter, quarter, 0))
        n2_q = jnp.stack(normed2_z)
        n2_x = swap_x(n2_q)
        n2_h = jnp.where(
            x_side == 0, jnp.concatenate([n2_q, n2_x], 1), jnp.concatenate([n2_x, n2_q], 1)
        )
        n2_o = swap_core(n2_h)
        x_all = rounded(jnp.concatenate([n2_h, n2_o], 1)).reshape(3 * row_count, width)
        og_h = jnp.stack(og_z)
        og_o = swap_core(og_h)
        og_all = rounded(jnp.concatenate([og_h, og_o], 1)).reshape(3 * row_count, width)
        gates_all = jnp.concatenate([local_order(v.T) for v in gates_z], 0)
        shard = width // dp_size

        def two_blocks(other, mine, rest):
            cut = lambda v, place: lax.dynamic_slice_in_dim(v, place * shard, shard, 1)
            return jnp.concatenate(
                [
                    jnp.concatenate([cut(v, place).T for v in (other, mine, rest)], 1)
                    for place in (dp_place, dp_place ^ 1)
                ],
                0,
            )

        xt = two_blocks(x_all, normed2_mine, normed2_other)
        ogt = two_blocks(og_all, og_mine, og_other)
        chunks = []
        for chunk in range(CHUNKS):
            kg, sg, ku, su, kd, sd = expert_grads(
                chunk, x_all, og_all, gates_all, xt, ogt, own_mine[:3], own_other[:3],
                w_gate, w_up, w_down,
            )
            chunks.append(
                [k + lax.ppermute(s, "dp", y_pairs) for k, s in ((kg, sg), (ku, su), (kd, sd))]
            )
        grad_w_gate, grad_w_up, grad_w_down = (
            jnp.concatenate([c[i] for c in chunks], 0) for i in range(3)
        )
    else:
        n2_own = jnp.concatenate([normed2_mine, normed2_other], 0)
        og_own = jnp.concatenate([og_mine, og_other], 0)
        ga, gg, ug = (
            jnp.concatenate([own_mine[i], own_other[i]], 0).reshape(row_count, EXPERTS, -1)
            for i in range(3)
        )
        grad_w_gate = jnp.einsum("td,tef->edf", n2_own, gg, preferred_element_type=wide)
        grad_w_up = jnp.einsum("td,tef->edf", n2_own, ug, preferred_element_type=wide)
        grad_w_down = jnp.einsum("tef,td->efd", ga, og_own, preferred_element_type=wide)
        grad_w_gate = lax.psum_scatter(grad_w_gate, "dp", scatter_dimension=1, tiled=True)
        grad_w_up = lax.psum_scatter(grad_w_up, "dp", scatter_dimension=1, tiled=True)
        grad_w_down = lax.psum_scatter(grad_w_down, "dp", scatter_dimension=2, tiled=True)

    grad_w_out = jnp.einsum("tc,td->cd", mixed_low, attn_grad, preferred_element_type=wide)
    mixed_grad = dot_nt(attn_grad, w_out).astype(bfloat)
    mixed_grad = mixed_grad.reshape(row_count, local_groups, per_group, HEAD_DIM)
    key_grad = jnp.zeros((row_count, local_groups, HEAD_DIM), wide)
    value_grad = jnp.zeros((row_count, local_groups, HEAD_DIM), wide)
    query_grads = []
    for block_num in range(block_count):
        row_start = block_num * block_rows
        scores, query_block = block_scores(block_num)
        soft = jnp.exp(scores - log_totals[block_num])
        grad_block = mixed_grad[row_start : row_start + block_rows]
        prob_grad = jnp.einsum("qgrd,kgd->grqk", grad_block, value_low, preferred_element_type=wide)
        row_dot = jnp.sum(soft * prob_grad, -1, keepdims=True)
        score_grad = (soft * (prob_grad - row_dot)).astype(bfloat)
        query_grads.append(
            jnp.einsum("grqk,kgd->qgrd", score_grad, key_low, preferred_element_type=wide)
            * scale_factor
        )
        key_grad = (
            key_grad
            + jnp.einsum("grqk,qgrd->kgd", score_grad, query_block, preferred_element_type=wide)
            * scale_factor
        )
        value_grad = value_grad + jnp.einsum(
            "grqk,qgrd->kgd", soft.astype(bfloat), grad_block, preferred_element_type=wide
        )
    query_rot_grad = jnp.concatenate(query_grads, 0).reshape(row_count, local_heads, HEAD_DIM)
    (query_in,) = query_back(query_rot_grad)
    (key_in,) = key_back(key_grad)
    qkv_low = jnp.concatenate(
        [
            query_in.astype(bfloat),
            key_in.astype(bfloat),
            value_grad.astype(bfloat).reshape(row_count, local_groups * HEAD_DIM),
        ],
        1,
    )
    w_qkv = jnp.concatenate([w_query, w_key, w_value], 1)
    normed1_grad = total_half(dot_nt(my_half(qkv_low), w_qkv), dot_nt(other_half(qkv_low), w_qkv))
    tokens_mine = my_half(tokens_wide)
    tokens_part, gain1_grad = norm_backward(tokens_mine, norm1_gain, normed1_grad)
    tokens_half = hidden_grad + tokens_part
    tokens_grad = natural(tokens_half, swap_core(tokens_half))

    grad_w_qkv = jnp.einsum("td,tc->dc", normed1_low, qkv_low, preferred_element_type=wide)
    grad_w_qkv = sum_blocks(grad_w_qkv.reshape(dp_size, width // dp_size, -1))
    grad_w_out = sum_blocks(
        grad_w_out.reshape(w_out.shape[0], dp_size, width // dp_size).transpose(1, 0, 2)
    )
    gain1 = sum_blocks((gain1_grad + swap_core(gain1_grad)).reshape(dp_size, -1))
    gain2 = sum_blocks((gain2_grad + swap_core(gain2_grad)).reshape(dp_size, -1))
    query_cols, key_cols = w_query.shape[1], w_key.shape[1]
    return (
        block_out,
        tokens_grad,
        gain1,
        grad_w_qkv[:, :query_cols],
        grad_w_qkv[:, query_cols : query_cols + key_cols],
        grad_w_qkv[:, query_cols + key_cols :],
        grad_w_out,
        gain2,
        grad_w_gate,
        grad_w_up,
        grad_w_down,
    )


def solution(mesh):
    placed = (
        P("dp", None),
        P("dp"),
        P("dp", None),
        P("dp", None),
        P(),
        P(None, "tensor"),
        P(None, "tensor"),
        P(None, "tensor"),
        P("tensor", None),
        P(),
        P(None, None, "tensor"),
        P(None, None, "tensor"),
        P(None, "tensor", None),
        P("dp", None),
    )
    return jax.shard_map(
        functools.partial(per_device, mesh.shape["dp"]),
        mesh=mesh,
        in_specs=placed,
        out_specs=(
            P("dp", None),
            P("dp", None),
            P("dp"),
            P("dp", "tensor"),
            P("dp", "tensor"),
            P("dp", "tensor"),
            P("tensor", "dp"),
            P("dp"),
            P(None, "dp", "tensor"),
            P(None, "dp", "tensor"),
            P(None, "tensor", "dp"),
        ),
        check_vma=False,
    )
```

time: 1970 us -> 944 us (0.48)
  waiting for transfers between devices: 1170 us -> 300 us
  local copies, waits for them, and re-layouts: 420 us -> 93 us
  Pallas kernels: 0 us -> 246 us
  matrix products: 243 us -> 56.7 us
  starting transfers between devices: 0.42 us -> 102 us
  other arithmetic: 93.1 us -> 131 us
  blocking collectives: 21.8 us -> 0 us
    reduce_scatter x7 -> x0, waiting for transfers between devices: 1080 us -> none  [the longest x1 286 us: per_device(): lax.psum_scatter(grad_w_down, 'dp', scatter_dimension=2, tiled=True)]
    ppermute x0 -> x63, waiting for transfers between devices: none -> 300 us  [the longest x9 139 us: along_z(): downs.append(lax.ppermute(downs[-1], 'dp', down_steps[k]))]
    gather x5 -> x0, local copies, waits for them, and re-layouts: 270 us -> none  [the longest x2 84.7 us: per_device(): normed2_low[slot_owner] * filled[:, None]]
    pallas_call x0 -> x6, Pallas kernels: none -> 246 us  [the longest x4 173 us: expert_grads(): pl.pallas_call(functools.partial(grads_body, first, other_rows), grid=(co...]
    dot_general x20 -> x11, matrix products: 220 us -> 34.6 us  [the longest x7 26.3 us: dot_nn(): return jnp.dot(a, b, preferred_element_type=wide)]
    scatter x3 -> x0, local copies, waits for them, and re-layouts: 130 us -> none  [the longest x1 56.6 us: per_device(): filled = jnp.zeros((EXPERTS * CAP,), bfloat).at[target].set(1.0)]
    ppermute x0 -> x63, starting transfers between devices: none -> 102 us  [the longest x12 45 us: sum_blocks(): lax.ppermute(part, 'dp', [(i, (i + 2 * k) % 8) for i in range(8)])]
    psum x3 -> x0, waiting for transfers between devices: 82.7 us -> none  [the longest x1 82.7 us: per_device(): expert_total = lax.psum(expert_part, 'tensor')]
  transfers between devices with their start and end apart: 10 -> 63, of which waited for: 8 -> 22; matrix products, arithmetic and copies ran while one was open for 20% -> 25% of each run, Pallas kernels for 0% -> 26%
where the time goes in v1:
time: 944 us; the launch traced here: 932 us
  waiting for transfers between devices  300 us (32%)
  Pallas kernels  246 us (26%)
  other arithmetic  131 us (14%)
  starting transfers between devices  102 us (11%)
  local copies, waits for them, and re-layouts  93 us (10%)
  matrix products  56.7 us (6%)
    pallas_call x4, Pallas kernels, expert_grads(): pl.pallas_call(functools.partial(grads_body, first, other_rows), grid=(co...  173 us
    ppermute x9, waiting for transfers between devices, along_z(): downs.append(lax.ppermute(downs[-1], 'dp', down_steps[k]))  139 us
    ppermute x12, waiting for transfers between devices, per_device(): lax.ppermute(s, 'dp', y_pairs)  93.1 us
    pallas_call x2, Pallas kernels, own_experts(): pl.pallas_call(own_body, grid=(experts // 2,), in_specs=[full((rows, widt...  73.7 us
    unnamed x267, local copies, waits for them, and re-layouts  46.6 us
    ppermute x12, starting transfers between devices, sum_blocks(): lax.ppermute(part, 'dp', [(i, (i + 2 * k) % 8) for i in range(8)])  45 us
    ppermute x5, waiting for transfers between devices, swap_x(): return lax.ppermute(v, 'tensor', X_PAIRS)  36.2 us
    dot_general x7, matrix products, dot_nn(): return jnp.dot(a, b, preferred_element_type=wide)  26.3 us
  transfers between devices with their start and end apart: 63, of which 22 were waited for; matrix products, arithmetic and copies ran while one was open for 25% of the time, Pallas kernels for 26%

profile of v1, /device:TPU:0, one launch (start us, length us, event | category | flops | bytes accessed | tf_op | source)
XLA Modules:
  0.0 932.1 jit_solution(15568381834576560325)
XLA Ops:
  58.5 25.5 %collective-permute-done.1 = f32[512,1024]{0,1:T(8,128)} collective-permute-done((f32[512,1024]{0,1:T(8,128)}, f32[512,1024]{0,1:T(8,128)}, u32[]{:S(2)}, u32[]{:S(2)}) %collective-permute-start.1) | collective-permute-done | bytes 2097184 | tf_op jit(solution)/shard_map/ppermute | solution.py:272
  93.6 13.9 %collective-permute-done.46 = f32[32,1024]{0,1:T(8,128)} collective-permute-done((f32[32,1024]{0,1:T(8,128)S(1)}, f32[32,1024]{0,1:T(8,128)}, u32[]{:S(2)}, u32[]{:S(2)}) %collective-permute-start.46) | collective-permute-done | bytes 131104 | tf_op jit(solution)/shard_map/ppermute | solution.py:294
  125.4 10.5 %collective-permute-done.48 = f32[32,1024]{0,1:T(8,128)S(1)} collective-permute-done((f32[32,1024]{0,1:T(8,128)}, f32[32,1024]{0,1:T(8,128)S(1)}, u32[]{:S(2)}, u32[]{:S(2)}) %collective-permute-start.48) | collective-permute-done | bytes 131104 | tf_op jit(solution)/shard_map/ppermute | solution.py:294
  153.1 36.9 %own_experts.3 = (bf16[512,4096]{1,0:T(8,128)(2,1)}, bf16[512,4096]{1,0:T(8,128)(2,1)}, bf16[512,4096]{1,0:T(8,128)(2,1)}, f32[512,1024]{1,0:T(8,128)S(1)}) custom-call(bf16[512,1024]{1,0:T(8,128)(2,1)S(1)} %copy-done.4, bf16[512,1024]{1,0:T(8,128)(2,1)S(1)} %get-tuple-element.140.og_ref, f32[512,32]{1,0:T(8,128)S(1)} %get-tuple-element.160.g_ref, ...), custom_call_target="tpu_custom_call" | custom-call | flops 21474836480 | bytes 37748736 | tf_op jit(solution)/shard_map/own_experts/pallas_call | solution.py:118
  194.2 10.6 %fusion.98 = f32[512,1024]{0,1:T(8,128)} fusion(bf16[512,4096]{1,0:T(8,128)(2,1)} %get-tuple-element.44.ga1_ref, bf16[4096,1024]{1,0:T(8,128)(2,1)} %bitcast.300), kind=kOutput, calls=%fused_computation.229 | convolution fusion | flops 4294967296 | bytes 14680064 | tf_op jit(solution)/shard_map/dot_general | solution.py:26
  212.4 36.8 %own_experts.2 = (bf16[512,4096]{1,0:T(8,128)(2,1)}, bf16[512,4096]{1,0:T(8,128)(2,1)}, bf16[512,4096]{1,0:T(8,128)(2,1)}, f32[512,1024]{1,0:T(8,128)S(1)}) custom-call(bf16[512,1024]{1,0:T(8,128)(2,1)S(1)} %copy.146.x_ref, bf16[512,1024]{1,0:T(8,128)(2,1)S(1)} %get-tuple-element.139.og_ref, f32[512,32]{1,0:T(8,128)S(1)} %get-tuple-element.159.g_ref, ...), custom_call_target="tpu_custom_call" | custom-call | flops 21474836480 | bytes 37748736 | tf_op jit(solution)/shard_map/own_experts/pallas_call | solution.py:118
  273.6 75.7 %collective-permute-done.33 = f32[256,1024]{0,1:T(8,128)S(1)} collective-permute-done((f32[256,1024]{0,1:T(8,128)}, f32[256,1024]{0,1:T(8,128)S(1)}, u32[]{:S(2)}, u32[]{:S(2)}) %collective-permute-start.33) | collective-permute-done | bytes 1048608 | tf_op jit(solution)/shard_map/ppermute | solution.py:294
  365.8 33.5 %collective-permute-done.41 = f32[512,1024]{0,1:T(8,128)} collective-permute-done((f32[512,1024]{0,1:T(8,128)}, f32[512,1024]{0,1:T(8,128)}, u32[]{:S(2)}, u32[]{:S(2)}) %collective-permute-start.41) | collective-permute-done | bytes 2097184 | tf_op jit(solution)/shard_map/ppermute | solution.py:294
  407.9 10.7 %collective-permute-done.36 = f32[3,256,1024]{1,2,0:T(8,128)} collective-permute-done((f32[3,256,1024]{1,2,0:T(8,128)S(1)}, f32[3,256,1024]{1,2,0:T(8,128)}, u32[]{:S(2)}, u32[]{:S(2)}) %collective-permute-start.36) | collective-permute-done | bytes 3145760 | tf_op jit(solution)/shard_map/ppermute | solution.py:272
  481.3 15.4 %collective-permute-done.21 = f32[4,256,128]{2,1,0:T(8,128)} collective-permute-done((f32[4,256,128]{2,1,0:T(8,128)S(1)}, f32[4,256,128]{2,1,0:T(8,128)}, u32[]{:S(2)}, u32[]{:S(2)}) %collective-permute-start.21) | collective-permute-done | bytes 524320 | tf_op jit(solution)/shard_map/ppermute | solution.py:304
  498.6 29.9 %collective-permute-start.24 = (f32[256,128]{1,0:T(8,128)}, f32[256,128]{1,0:T(8,128)}, u32[]{:S(2)}, u32[]{:S(2)}) collective-permute-start(f32[256,128]{1,0:T(8,128)} %get-tuple-element.153), channel_id=1, source_target_pairs={{0,24},{4,28},{8,0},{12,4},{16,8},{20,12},{24,16},{28,20},{1,25},{... | collective-permute-start | bytes 393224 | tf_op jit(solution)/shard_map/ppermute | solution.py:308
  569.4 9.9 %maximum_maximum_fusion.1.ogt_ref = bf16[256,4096]{1,0:T(8,128)(2,1)} fusion(bf16[128,512]{1,0:T(8,128)(2,1)S(1)} %bitcast.290, bf16[128,512]{1,0:T(8,128)(2,1)S(1)} %bitcast.291, bf16[128,3072]{1,0:T(8,128)(2,1)S(1)} %bitcast.256, bf16[128,512]{1,0:T(8,128)(2,1)S(1)} %bitcast.292, bf16[128,512]{1,0:T(8,128)(2,1)S(1)} %bitcast.293, ...), kind=kLoop, calls=%fused_computation.41 | loop fusion | flops 12582912 | bytes 4194304 | tf_op jit(solution)/shard_map/concatenate | solution.py:411
  579.3 43.1 %expert_grads.7 = (f32[8,128,128]{2,1,0:T(8,128)}, f32[8,128,128]{2,1,0:T(8,128)}, f32[8,128,128]{2,1,0:T(8,128)}, f32[8,128,128]{2,1,0:T(8,128)}, f32[8,128,128]{2,1,0:T(8,128)}, /*index=5*/f32[8,128,128]{2,1,0:T(8,128)}) custom-call(bf16[3072,1024]{1,0:T(8,128)(2,1)} %bitcast.247, bf16[3072,1024]{1,0:T(8,128)(2,1)} %bitcast.242, ...), custom_call_target="tpu_custom_call" | custom-call | flops 25769803776 | bytes 18874368 | tf_op jit(solution)/shard_map/expert_grads/pallas_call | solution.py:209
  622.4 43.4 %expert_grads.6 = (f32[8,128,128]{2,1,0:T(8,128)}, f32[8,128,128]{2,1,0:T(8,128)}, f32[8,128,128]{2,1,0:T(8,128)}, f32[8,128,128]{2,1,0:T(8,128)}, f32[8,128,128]{2,1,0:T(8,128)}, /*index=5*/f32[8,128,128]{2,1,0:T(8,128)}) custom-call(bf16[3072,1024]{1,0:T(8,128)(2,1)} %bitcast.248, bf16[3072,1024]{1,0:T(8,128)(2,1)} %bitcast.243, ...), custom_call_target="tpu_custom_call" | custom-call | flops 25769803776 | bytes 18874368 | tf_op jit(solution)/shard_map/expert_grads/pallas_call | solution.py:209
  668.2 43.1 %expert_grads.5 = (f32[8,128,128]{2,1,0:T(8,128)}, f32[8,128,128]{2,1,0:T(8,128)}, f32[8,128,128]{2,1,0:T(8,128)}, f32[8,128,128]{2,1,0:T(8,128)}, f32[8,128,128]{2,1,0:T(8,128)}, /*index=5*/f32[8,128,128]{2,1,0:T(8,128)}) custom-call(bf16[3072,1024]{1,0:T(8,128)(2,1)} %bitcast.249, bf16[3072,1024]{1,0:T(8,128)(2,1)} %bitcast.244, ...), custom_call_target="tpu_custom_call" | custom-call | flops 25769803776 | bytes 18874368 | tf_op jit(solution)/shard_map/expert_grads/pallas_call | solution.py:209
  712.9 43.1 %expert_grads.4 = (f32[8,128,128]{2,1,0:T(8,128)}, f32[8,128,128]{2,1,0:T(8,128)}, f32[8,128,128]{2,1,0:T(8,128)}, f32[8,128,128]{2,1,0:T(8,128)}, f32[8,128,128]{2,1,0:T(8,128)}, /*index=5*/f32[8,128,128]{2,1,0:T(8,128)}) custom-call(bf16[3072,1024]{1,0:T(8,128)(2,1)} %bitcast.250, bf16[3072,1024]{1,0:T(8,128)(2,1)} %bitcast.245, ...), custom_call_target="tpu_custom_call" | custom-call | flops 25769803776 | bytes 18874368 | tf_op jit(solution)/shard_map/expert_grads/pallas_call | solution.py:209
  763.2 11.5 %collective-permute-done.23 = f32[256,128]{1,0:T(8,128)S(1)} collective-permute-done((f32[256,128]{1,0:T(8,128)S(1)}, f32[256,128]{1,0:T(8,128)S(1)}, u32[]{:S(2)}, u32[]{:S(2)}) %collective-permute-start.23) | collective-permute-done | bytes 131104 | tf_op jit(solution)/shard_map/ppermute | solution.py:308
  795.5 10.8 %collective-permute-done.53 = f32[8,128,128]{2,1,0:T(8,128)} collective-permute-done((f32[8,128,128]{2,1,0:T(8,128)}, f32[8,128,128]{2,1,0:T(8,128)}, u32[]{:S(2)}, u32[]{:S(2)}) %collective-permute-start.53) | collective-permute-done | bytes 524320 | tf_op jit(solution)/shard_map/ppermute | solution.py:428
  806.8 10.7 %collective-permute-done.52 = f32[8,128,128]{2,1,0:T(8,128)} collective-permute-done((f32[8,128,128]{2,1,0:T(8,128)}, f32[8,128,128]{2,1,0:T(8,128)}, u32[]{:S(2)}, u32[]{:S(2)}) %collective-permute-start.52) | collective-permute-done | bytes 524320 | tf_op jit(solution)/shard_map/ppermute | solution.py:428
  818.0 10.7 %collective-permute-done.51 = f32[8,128,128]{2,1,0:T(8,128)} collective-permute-done((f32[8,128,128]{2,1,0:T(8,128)}, f32[8,128,128]{2,1,0:T(8,128)}, u32[]{:S(2)}, u32[]{:S(2)}) %collective-permute-start.51) | collective-permute-done | bytes 524320 | tf_op jit(solution)/shard_map/ppermute | solution.py:428
  851.7 10.7 %collective-permute-done.56 = f32[8,128,128]{2,1,0:T(8,128)} collective-permute-done((f32[8,128,128]{2,1,0:T(8,128)}, f32[8,128,128]{2,1,0:T(8,128)}, u32[]{:S(2)}, u32[]{:S(2)}) %collective-permute-start.56) | collective-permute-done | bytes 524320 | tf_op jit(solution)/shard_map/ppermute | solution.py:428
  863.0 10.7 %collective-permute-done.55 = f32[8,128,128]{2,1,0:T(8,128)} collective-permute-done((f32[8,128,128]{2,1,0:T(8,128)}, f32[8,128,128]{2,1,0:T(8,128)}, u32[]{:S(2)}, u32[]{:S(2)}) %collective-permute-start.55) | collective-permute-done | bytes 524320 | tf_op jit(solution)/shard_map/ppermute | solution.py:428
  885.8 10.2 %collective-permute-done.61 = f32[8,128,128]{2,1,0:T(8,128)S(1)} collective-permute-done((f32[8,128,128]{2,1,0:T(8,128)}, f32[8,128,128]{2,1,0:T(8,128)S(1)}, u32[]{:S(2)}, u32[]{:S(2)}) %collective-permute-start.61) | collective-permute-done | bytes 524320 | tf_op jit(solution)/shard_map/ppermute | solution.py:428
  896.1 11.2 %collective-permute-done.60 = f32[8,128,128]{2,1,0:T(8,128)S(1)} collective-permute-done((f32[8,128,128]{2,1,0:T(8,128)}, f32[8,128,128]{2,1,0:T(8,128)S(1)}, u32[]{:S(2)}, u32[]{:S(2)}) %collective-permute-start.60) | collective-permute-done | bytes 524320 | tf_op jit(solution)/shard_map/ppermute | solution.py:428
  (515 shorter events, 360.8 us)
Async XLA Ops:
  42.2 162.6 %collective-permute-start.38 = (f32[512,1024]{0,1:T(8,128)}, f32[512,1024]{0,1:T(8,128)}, u32[]{:S(2)}, u32[]{:S(2)}) collective-permute-start(f32[512,1024]{0,1:T(8,128)} %convert_element_type.98), channel_id=1, source_target_pairs={{0,8},{4,12},{8,16},{12,20},{16,24},{20,28},{1,9},{5,13},{9,17},{1... | collective-permute-start | bytes 6291464 | tf_op jit(solution)/shard_map/ppermute | solution.py:293
  47.0 160.5 %collective-permute-start.39 = (f32[512,1024]{0,1:T(8,128)}, f32[512,1024]{0,1:T(8,128)}, u32[]{:S(2)}, u32[]{:S(2)}) collective-permute-start(f32[512,1024]{0,1:T(8,128)} %convert_element_type.98), channel_id=1, source_target_pairs={{8,0},{12,4},{16,8},{20,12},{24,16},{28,20},{9,1},{13,5},{17,9},{2... | collective-permute-start | bytes 6291464 | tf_op jit(solution)/shard_map/ppermute | solution.py:294
  48.7 60.2 %collective-permute-start.45 = (f32[32,1024]{0,1:T(8,128)S(1)}, f32[32,1024]{0,1:T(8,128)}, u32[]{:S(2)}, u32[]{:S(2)}) collective-permute-start(f32[32,1024]{0,1:T(8,128)S(1)} %bitcast.270), channel_id=1, source_target_pairs={{0,8},{4,12},{8,16},{12,20},{16,24},{20,28},{1,9},{5,13},{9,17},{1... | collective-permute-start | bytes 393224 | tf_op jit(solution)/shard_map/ppermute | solution.py:293
  141.5 68.0 %collective-permute-start.30 = (f32[256,1024]{0,1:T(8,128)}, f32[256,1024]{0,1:T(8,128)}, u32[]{:S(2)}, u32[]{:S(2)}) collective-permute-start(f32[256,1024]{0,1:T(8,128)} %constant_dynamic-slice_fusion.4), channel_id=1, source_target_pairs={{0,8},{4,12},{8,16},{12,20},{16,24},{20,28},{1,9},{5,13},{9,17},{1... | collective-permute-start | bytes 3145736 | tf_op jit(solution)/shard_map/ppermute | solution.py:293
  145.1 66.1 %collective-permute-start.31 = (f32[256,1024]{0,1:T(8,128)}, f32[256,1024]{0,1:T(8,128)}, u32[]{:S(2)}, u32[]{:S(2)}) collective-permute-start(f32[256,1024]{0,1:T(8,128)} %constant_dynamic-slice_fusion.4), channel_id=1, source_target_pairs={{8,0},{12,4},{16,8},{20,12},{24,16},{28,20},{9,1},{13,5},{17,9},{2... | collective-permute-start | bytes 3145736 | tf_op jit(solution)/shard_map/ppermute | solution.py:294
  194.2 60.4 %collective-permute-start.6 = (f32[512,1024]{0,1:T(8,128)}, f32[512,1024]{0,1:T(8,128)}, u32[]{:S(2)}, u32[]{:S(2)}) collective-permute-start(f32[512,1024]{0,1:T(8,128)} %copy.152), channel_id=1, source_target_pairs={{0,1},{1,0},{2,3},{3,2},{4,5},{5,4},{6,7},{7,6},{8,9},{9,8},{10,11... | collective-permute-start | bytes 6291464 | tf_op jit(solution)/shard_map/ppermute | solution.py:269
  207.5 60.9 %collective-permute-start.42 = (f32[512,1024]{0,1:T(8,128)}, f32[512,1024]{0,1:T(8,128)}, u32[]{:S(2)}, u32[]{:S(2)}) collective-permute-start(f32[512,1024]{0,1:T(8,128)} %collective-permute-done.38), channel_id=1, source_target_pairs={{8,16},{12,20},{16,24},{20,28},{9,17},{13,21},{17,25},{21,29},{10,... | collective-permute-start | bytes 6291464 | tf_op jit(solution)/shard_map/ppermute | solution.py:293
  252.5 98.5 %collective-permute-start.40 = (f32[512,1024]{0,1:T(8,128)}, f32[512,1024]{0,1:T(8,128)}, u32[]{:S(2)}, u32[]{:S(2)}) collective-permute-start(f32[512,1024]{0,1:T(8,128)} %collective-permute-done.39), channel_id=1, source_target_pairs={{8,0},{12,4},{16,8},{20,12},{9,1},{13,5},{17,9},{21,13},{10,2},{14... | collective-permute-start | bytes 6291464 | tf_op jit(solution)/shard_map/ppermute | solution.py:294
  254.6 94.7 %collective-permute-start.33 = (f32[256,1024]{0,1:T(8,128)}, f32[256,1024]{0,1:T(8,128)S(1)}, u32[]{:S(2)}, u32[]{:S(2)}) collective-permute-start(f32[256,1024]{0,1:T(8,128)} %collective-permute-done.32), channel_id=1, source_target_pairs={{8,0},{12,4},{9,1},{13,5},{10,2},{14,6},{11,3},{15,7}} | collective-permute-start | bytes 3145736 | tf_op jit(solution)/shard_map/ppermute | solution.py:294
  258.1 96.7 %collective-permute-start.7 = (f32[512,1024]{0,1:T(8,128)S(1)}, f32[512,1024]{0,1:T(8,128)S(1)}, u32[]{:S(2)}, u32[]{:S(2)}) collective-permute-start(f32[512,1024]{0,1:T(8,128)S(1)} %add.362), channel_id=1, source_target_pairs={{0,2},{1,3},{2,0},{3,1},{4,6},{5,7},{6,4},{7,5},{8,10},{9,11},{10,... | collective-permute-start | bytes 6291464 | tf_op jit(solution)/shard_map/ppermute | solution.py:272
  268.4 87.2 %collective-permute-start.4 = (f32[512,1024]{0,1:T(8,128)S(1)}, f32[512,1024]{0,1:T(8,128)S(1)}, u32[]{:S(2)}, u32[]{:S(2)}) collective-permute-start(f32[512,1024]{0,1:T(8,128)S(1)} %convolution_add_fusion.2), channel_id=1, source_target_pairs={{0,2},{1,3},{2,0},{3,1},{4,6},{5,7},{6,4},{7,5},{8,10},{9,11},{10,... | collective-permute-start | bytes 6291464 | tf_op jit(solution)/shard_map/ppermute | solution.py:272
  271.4 92.3 %collective-permute-start.43 = (f32[512,1024]{0,1:T(8,128)}, f32[512,1024]{0,1:T(8,128)S(1)}, u32[]{:S(2)}, u32[]{:S(2)}) collective-permute-start(f32[512,1024]{0,1:T(8,128)} %collective-permute-done.42), channel_id=1, source_target_pairs={{16,24},{20,28},{17,25},{21,29},{18,26},{22,30},{19,27},{23,31}} | collective-permute-start | bytes 6291464 | tf_op jit(solution)/shard_map/ppermute | solution.py:293
  349.7 68.9 %collective-permute-start.36 = (f32[3,256,1024]{1,2,0:T(8,128)S(1)}, f32[3,256,1024]{1,2,0:T(8,128)}, u32[]{:S(2)}, u32[]{:S(2)}) collective-permute-start(f32[3,256,1024]{1,2,0:T(8,128)S(1)} %pad_maximum_fusion.1), channel_id=1, source_target_pairs={{0,2},{1,3},{2,0},{3,1},{4,6},{5,7},{6,4},{7,5},{8,10},{9,11},{10,... | collective-permute-start | bytes 9437192 | tf_op jit(solution)/shard_map/ppermute | solution.py:272
  360.8 63.5 %collective-permute-start.8 = (f32[512,1024]{0,1:T(8,128)S(1)}, f32[512,1024]{0,1:T(8,128)S(1)}, u32[]{:S(2)}, u32[]{:S(2)}) collective-permute-start(f32[512,1024]{0,1:T(8,128)S(1)} %get-tuple-element.124), channel_id=1, source_target_pairs={{0,1},{1,0},{2,3},{3,2},{4,5},{5,4},{6,7},{7,6},{8,9},{9,8},{10,11... | collective-permute-start | bytes 6291464 | tf_op jit(solution)/shard_map/ppermute | solution.py:269
  405.6 57.9 %collective-permute-start.44 = (f32[3,512,1024]{1,2,0:T(8,128)}, f32[3,512,1024]{1,2,0:T(8,128)}, u32[]{:S(2)}, u32[]{:S(2)}) collective-permute-start(f32[3,512,1024]{1,2,0:T(8,128)} %pad_maximum_fusion), channel_id=1, source_target_pairs={{0,1},{1,0},{2,3},{3,2},{4,5},{5,4},{6,7},{7,6},{8,9},{9,8},{10,11... | collective-permute-start | bytes 18874376 | tf_op jit(solution)/shard_map/ppermute | solution.py:269
  407.4 348.7 %collective-permute-start.5 = (f32[512,1024]{0,1:T(8,128)}, f32[512,1024]{0,1:T(8,128)}, u32[]{:S(2)}, u32[]{:S(2)}) collective-permute-start(f32[512,1024]{0,1:T(8,128)} %get-tuple-element.138), channel_id=1, source_target_pairs={{0,1},{1,0},{2,3},{3,2},{4,5},{5,4},{6,7},{7,6},{8,9},{9,8},{10,11... | collective-permute-start | bytes 6291464 | tf_op jit(solution)/shard_map/ppermute | solution.py:269
  423.7 112.3 %collective-permute-start.37 = (f32[3,512,1024]{1,2,0:T(8,128)}, f32[3,512,1024]{1,2,0:T(8,128)}, u32[]{:S(2)}, u32[]{:S(2)}) collective-permute-start(f32[3,512,1024]{1,2,0:T(8,128)} %maximum_select_fusion), channel_id=1, source_target_pairs={{0,1},{1,0},{2,3},{3,2},{4,5},{5,4},{6,7},{7,6},{8,9},{9,8},{10,11... | collective-permute-start | bytes 18874376 | tf_op jit(solution)/shard_map/ppermute | solution.py:269
  457.2 76.1 %collective-permute-start.9 = (f32[512,1024]{0,1:T(8,128)}, f32[512,1024]{0,1:T(8,128)}, u32[]{:S(2)}, u32[]{:S(2)}) collective-permute-start(f32[512,1024]{0,1:T(8,128)} %fusion.50), channel_id=1, source_target_pairs={{0,1},{1,0},{2,3},{3,2},{4,5},{5,4},{6,7},{7,6},{8,9},{9,8},{10,11... | collective-permute-start | bytes 6291464 | tf_op jit(solution)/shard_map/ppermute | solution.py:269
  460.1 68.4 %collective-permute-start.17 = (f32[4,128,512]{2,1,0:T(8,128)}, f32[4,128,512]{2,1,0:T(8,128)}, u32[]{:S(2)}, u32[]{:S(2)}) collective-permute-start(f32[4,128,512]{2,1,0:T(8,128)} %dynamic-slice_bitcast_fusion), channel_id=1, source_target_pairs={{0,4},{4,0},{8,12},{12,8},{16,20},{20,16},{24,28},{28,24},{1,5},{5... | collective-permute-start | bytes 3145736 | tf_op jit(solution)/shard_map/ppermute | solution.py:304
  498.6 258.9 %collective-permute-start.24 = (f32[256,128]{1,0:T(8,128)}, f32[256,128]{1,0:T(8,128)}, u32[]{:S(2)}, u32[]{:S(2)}) collective-permute-start(f32[256,128]{1,0:T(8,128)} %get-tuple-element.153), channel_id=1, source_target_pairs={{0,24},{4,28},{8,0},{12,4},{16,8},{20,12},{24,16},{28,20},{1,25},{... | collective-permute-start | bytes 393224 | tf_op jit(solution)/shard_map/ppermute | solution.py:308
  530.9 245.0 %collective-permute-start.20 = (f32[128,512]{1,0:T(8,128)}, f32[128,512]{1,0:T(8,128)}, u32[]{:S(2)}, u32[]{:S(2)}) collective-permute-start(f32[128,512]{1,0:T(8,128)} %get-tuple-element.146), channel_id=1, source_target_pairs={{0,24},{4,28},{8,0},{12,4},{16,8},{20,12},{24,16},{28,20},{1,25},{... | collective-permute-start | bytes 786440 | tf_op jit(solution)/shard_map/ppermute | solution.py:308
  533.3 243.5 %collective-permute-start.19 = (f32[128,512]{1,0:T(8,128)}, f32[128,512]{1,0:T(8,128)}, u32[]{:S(2)}, u32[]{:S(2)}) collective-permute-start(f32[128,512]{1,0:T(8,128)} %get-tuple-element.147), channel_id=1, source_target_pairs={{0,16},{4,20},{8,24},{12,28},{16,0},{20,4},{24,8},{28,12},{1,17},{... | collective-permute-start | bytes 786440 | tf_op jit(solution)/shard_map/ppermute | solution.py:308
  536.0 129.9 %collective-permute-start.10 = (f32[512,1024]{0,1:T(8,128)S(1)}, f32[512,1024]{0,1:T(8,128)}, u32[]{:S(2)}, u32[]{:S(2)}) collective-permute-start(f32[512,1024]{0,1:T(8,128)S(1)} %convolution_add_fusion), channel_id=1, source_target_pairs={{0,2},{1,3},{2,0},{3,1},{4,6},{5,7},{6,4},{7,5},{8,10},{9,11},{10,... | collective-permute-start | bytes 6291464 | tf_op jit(solution)/shard_map/ppermute | solution.py:272
  790.8 130.2 %collective-permute-start.11 = (f32[512,1024]{0,1:T(8,128)}, f32[512,1024]{0,1:T(8,128)S(1)}, u32[]{:S(2)}, u32[]{:S(2)}) collective-permute-start(f32[512,1024]{0,1:T(8,128)} %subtract_add_fusion), channel_id=1, source_target_pairs={{0,1},{1,0},{2,3},{3,2},{4,5},{5,4},{6,7},{7,6},{8,9},{9,8},{10,11... | collective-permute-start | bytes 6291464 | tf_op jit(solution)/shard_map/ppermute | solution.py:269
  (163 other events, 2541.4 us)

commit v2 on v1

v2 whole, which is shorter than its diff:
```python
import functools

import jax
import jax.numpy as jnp
from jax import lax
from jax.experimental import pallas as pl
from jax.experimental.pallas import tpu as pltpu
from jax.sharding import PartitionSpec as P

HEAD_DIM = 64
EXPERTS = 32
TOP = 8
EPS = 1e-06
ROPE_BASE = 10000.0
CHUNK_SIZES = (8, 8, 8, 8)

bfloat = jnp.bfloat16
wide = jnp.float32

BRIEF = pl.CostEstimate(flops=2**20, bytes_accessed=2**20, transcendentals=0)

CORE_PAIRS = [(i, i ^ 1) for i in range(4)]
X_PAIRS = [(i, i ^ 2) for i in range(4)]


def dot_nn(a, b):
    return jnp.dot(a, b, preferred_element_type=wide)


def dot_nt(a, b):
    return lax.dot_general(a, b, (((1,), (1,)), ((), ())), preferred_element_type=wide)


def norm_forward(v, gain):
    return v * lax.rsqrt(jnp.mean(v * v, -1, keepdims=True) + EPS) * gain


def norm_backward(v, gain, q):
    r = lax.rsqrt(jnp.mean(v * v, -1, keepdims=True) + EPS)
    gq = gain * q
    v_grad = r * gq - v * (r * r * r) * jnp.mean(v * gq, -1, keepdims=True)
    return v_grad, jnp.sum(q * v * r, 0)


def rope_tables(positions):
    half_dim = HEAD_DIM // 2
    freqs = ROPE_BASE ** (-(jnp.arange(half_dim, dtype=jnp.float32) * 2.0) / HEAD_DIM)
    angles = positions.astype(jnp.float32)[:, None] * freqs[None, :]
    cosine = jnp.cos(angles)
    sine_table = jnp.sin(angles)
    return (jnp.concatenate([cosine, cosine], -1), jnp.concatenate([sine_table, sine_table], -1))


def rotate(values_in, cosine, sine_table):
    half_dim = values_in.shape[-1] // 2
    turned = jnp.concatenate([-values_in[..., half_dim:], values_in[..., :half_dim]], -1)
    return values_in * cosine[:, None, :] + turned * sine_table[:, None, :]


def expert_parts(x, og, gate_cols, w_pair, wd2):
    hidden = wd2.shape[0] // 2
    back = dot_nt(og, wd2)
    out = []
    for j in range(2):
        both = dot_nn(x, w_pair[j])
        gate, up = both[:, :hidden], both[:, hidden:]
        col = gate_cols[j]
        sig = 0.5 * jnp.tanh(0.5 * gate) + 0.5
        act = gate * sig
        slope = sig + act * (1.0 - sig)
        weighted = back[:, j * hidden : (j + 1) * hidden] * col
        out.append(
            (
                (act * up * col).astype(bfloat),
                (weighted * up * slope).astype(bfloat),
                (weighted * act).astype(bfloat),
            )
        )
    return out


def gate_columns(g, first):
    lane = lax.broadcasted_iota(jnp.int32, g.shape, 1)
    return [
        jnp.sum(jnp.where(lane == first + j, g, 0.0), axis=1, keepdims=True) for j in range(2)
    ]


def own_body(x_ref, og_ref, g_ref, wg_ref, wu_ref, wd_ref, ga_ref, gu_ref, n_ref):
    pair = pl.program_id(0)
    hidden = wg_ref.shape[2]

    @pl.when(pair == 0)
    def _():
        n_ref[...] = jnp.zeros_like(n_ref)

    w_pair = [jnp.concatenate([wg_ref[j], wu_ref[j]], axis=1) for j in range(2)]
    wd2 = wd_ref[...].reshape(2 * hidden, wd_ref.shape[2])
    cols = gate_columns(g_ref[...], 2 * pair)
    parts = expert_parts(x_ref[...], og_ref[...], cols, w_pair, wd2)
    total = n_ref[...]
    for j in range(2):
        ga, gg, ug = parts[j]
        ga_ref[:, j * hidden : (j + 1) * hidden] = ga
        gu = jnp.concatenate([gg, ug], axis=1)
        gu_ref[:, 2 * j * hidden : 2 * (j + 1) * hidden] = gu
        total = total + dot_nt(gu, w_pair[j])
    n_ref[...] = total


def whole(a):
    return pl.BlockSpec(a.shape, lambda *_: (0,) * a.ndim, pipeline_mode=pl.Buffered(1))


def own_experts(x, og, g, w_gate, w_up, w_down):
    rows, width = x.shape
    experts, _, hidden = w_gate.shape
    up_spec = pl.BlockSpec((2, width, hidden), lambda p: (p, 0, 0))
    return pl.pallas_call(
        own_body,
        grid=(experts // 2,),
        in_specs=[
            whole(x),
            whole(og),
            whole(g),
            up_spec,
            up_spec,
            pl.BlockSpec((2, hidden, width), lambda p: (p, 0, 0)),
        ],
        out_specs=[
            pl.BlockSpec((rows, 2 * hidden), lambda p: (0, p)),
            pl.BlockSpec((rows, 4 * hidden), lambda p: (0, p)),
            pl.BlockSpec((rows, width), lambda p: (0, 0)),
        ],
        out_shape=[
            jax.ShapeDtypeStruct((rows, experts * hidden), bfloat),
            jax.ShapeDtypeStruct((rows, 2 * experts * hidden), bfloat),
            jax.ShapeDtypeStruct((rows, width), wide),
        ],
        compiler_params=pltpu.CompilerParams(
            dimension_semantics=("arbitrary",), vmem_limit_bytes=40 * 2**20
        ),
        cost_estimate=BRIEF,
        name="own_experts",
    )(x, og, g, w_gate, w_up, w_down)


def grads_body(first, parts_n, *refs):
    x_refs, og_refs, g_refs, xt_refs, ogt_refs = (
        refs[parts_n * i : parts_n * (i + 1)] for i in range(5)
    )
    own_xt, own_ogt, own_ga, own_gu, wg_ref, wu_ref, wd_ref, keep, send = refs[
        5 * parts_n : 5 * parts_n + 9
    ]
    s_refs, sa_ref = refs[-3:-1], refs[-1]
    pair = pl.program_id(0)
    hidden = wg_ref.shape[2]
    w_pair = [jnp.concatenate([wg_ref[j], wu_ref[j]], axis=1) for j in range(2)]
    wd2 = wd_ref[...].reshape(2 * hidden, wd_ref.shape[2])
    rows = x_refs[0].shape[0]

    for n in range(parts_n):
        to = slice(n * rows, (n + 1) * rows)
        cols = gate_columns(g_refs[n][...], 2 * (pair + first))
        parts = expert_parts(x_refs[n][...], og_refs[n][...], cols, w_pair, wd2)
        for j in range(2):
            ga, gg, ug = parts[j]
            sa_ref[to, j * hidden : (j + 1) * hidden] = ga
            s_refs[j][to, :hidden] = gg
            s_refs[j][to, hidden:] = ug

    def total(transposed, own_transposed, scratch, own):
        out = dot_nn(own_transposed[...], own)
        for n in range(parts_n):
            out = out + dot_nn(transposed[n][...], scratch[n * rows : (n + 1) * rows])
        return out

    shard = own_xt.shape[0] // 2
    for j in range(2):
        lanes = slice(2 * j * hidden, 2 * (j + 1) * hidden)
        grad = total(xt_refs, own_xt, s_refs[j], own_gu[:, lanes])
        for i in range(2):
            keep[j, i] = grad[:shard, i * hidden : (i + 1) * hidden]
            send[j, i] = grad[shard:, i * hidden : (i + 1) * hidden]
    down = total(ogt_refs, own_ogt, sa_ref, own_ga[...])
    for j in range(2):
        turned = down[:, j * hidden : (j + 1) * hidden].T
        keep[j, 2] = turned[:, :shard]
        send[j, 2] = turned[:, shard:]


def expert_grads(first_expert, count, x, og, g, xt, ogt, own_xt, own_ogt, own_ga, own_gu, weights):
    rows, width = x[0].shape
    w_gate, w_up, w_down = weights
    _, _, hidden = w_gate.shape
    own_rows = own_ga.shape[0]
    all_rows = len(x) * rows
    shard = own_xt.shape[0] // 2
    first = first_expert // 2
    up_spec = pl.BlockSpec((2, width, hidden), lambda p: (p + first, 0, 0))
    out_spec = pl.BlockSpec((2, 3, shard, hidden), lambda p: (p, 0, 0, 0))
    out_shape = jax.ShapeDtypeStruct((count, 3, shard, hidden), wide)
    resident = (*x, *og, *g, *xt, *ogt, own_xt, own_ogt)
    return pl.pallas_call(
        functools.partial(grads_body, first, len(x)),
        grid=(count // 2,),
        in_specs=[whole(a) for a in resident]
        + [pl.BlockSpec((own_rows, 2 * hidden), lambda p: (0, p + first))]
        + [pl.BlockSpec((own_rows, 4 * hidden), lambda p: (0, p + first))]
        + [up_spec, up_spec, pl.BlockSpec((2, hidden, width), lambda p: (p + first, 0, 0))],
        out_specs=[out_spec] * 2,
        out_shape=[out_shape] * 2,
        scratch_shapes=[pltpu.VMEM((all_rows, 2 * hidden), bfloat)] * 3,
        compiler_params=pltpu.CompilerParams(
            dimension_semantics=("arbitrary",), vmem_limit_bytes=56 * 2**20
        ),
        cost_estimate=BRIEF,
        name="expert_grads",
    )(*resident, own_ga, own_gu, *weights)


def prepare_body(normed, place_ref, mine_ref, other_ref, gain_ref, x_ref, t_ref):
    shard = t_ref.shape[0] // 2
    blocks = pl.num_programs(0) // 2

    def emit(v_ref):
        v = v_ref[...]
        if normed:
            scale = lax.rsqrt(jnp.mean(v * v, -1, keepdims=True) + EPS)
            v = v * scale * gain_ref[...]
        x_ref[...] = v.astype(bfloat)
        for i in range(2):
            cols = pl.ds(pl.multiple_of((place_ref[0] ^ i) * shard, shard), shard)
            cut = v_ref[:, cols]
            if normed:
                cut = cut * scale * gain_ref[:, cols]
            t_ref[i * shard : (i + 1) * shard, :] = cut.T.astype(bfloat)

    @pl.when(pl.program_id(0) < blocks)
    def _():
        emit(mine_ref)

    @pl.when(pl.program_id(0) >= blocks)
    def _():
        emit(other_ref)


def prepare(mine, other, gain, place, shard, half, normed):
    width = mine.shape[1]
    block = 256
    blocks = half // block
    return pl.pallas_call(
        functools.partial(prepare_body, normed),
        grid_spec=pltpu.PrefetchScalarGridSpec(
            num_scalar_prefetch=1,
            grid=(2 * blocks,),
            in_specs=[
                pl.BlockSpec((block, width), lambda i, _: (jnp.minimum(i, blocks - 1), 0)),
                pl.BlockSpec((block, width), lambda i, _: (jnp.maximum(i - blocks, 0), 0)),
                pl.BlockSpec((1, width), lambda i, _: (0, 0)),
            ],
            out_specs=[
                pl.BlockSpec((block, width), lambda i, _: (i, 0)),
                pl.BlockSpec((2 * shard, block), lambda i, _: (0, i)),
            ],
        ),
        out_shape=[
            jax.ShapeDtypeStruct((2 * half, width), bfloat),
            jax.ShapeDtypeStruct((2 * shard, 2 * half), bfloat),
        ],
        cost_estimate=BRIEF,
        name="prepare",
    )(place.reshape(1), mine, other, gain.reshape(1, width))


def place_halves_body(core_ref, mine_ref, other_ref, out_ref):
    half = pl.program_id(0)

    @pl.when(half == 0)
    def _():
        out_ref[...] = mine_ref[...]

    @pl.when(half == 1)
    def _():
        out_ref[...] = other_ref[...]


def place_halves(mine, other, core):
    rows, width = mine.shape
    steps = 2
    block = (rows // steps, width)
    return pl.pallas_call(
        place_halves_body,
        grid_spec=pltpu.PrefetchScalarGridSpec(
            num_scalar_prefetch=1,
            grid=(2, steps),
            in_specs=[
                pl.BlockSpec(block, lambda h, i, _: (jnp.where(h == 0, i, steps - 1), 0)),
                pl.BlockSpec(block, lambda h, i, _: (jnp.where(h == 0, 0, i), 0)),
            ],
            out_specs=pl.BlockSpec(block, lambda h, i, c: ((h ^ c[0]) * steps + i, 0)),
        ),
        out_shape=jax.ShapeDtypeStruct((2 * rows, width), mine.dtype),
        cost_estimate=BRIEF,
        name="place_halves",
    )(core.reshape(1), mine, other)


def after(v, *others):
    return lax.optimization_barrier((v, *others))[0]


def together(*values):
    return lax.optimization_barrier(values)


def per_device(
    dp_size,
    tokens,
    positions,
    routes,
    gates,
    norm1_gain,
    w_query,
    w_key,
    w_value,
    w_out,
    norm2_gain,
    w_gate,
    w_up,
    w_down,
    out_grad,
):
    row_count, width = tokens.shape
    half = row_count // 2
    local_heads = w_query.shape[1] // HEAD_DIM
    local_groups = w_key.shape[1] // HEAD_DIM
    per_group = local_heads // local_groups
    scale_factor = HEAD_DIM ** (-0.5)
    block_rows = min(512, row_count)
    block_count = row_count // block_rows
    core = lax.axis_index("tensor") % 2
    x_side = lax.axis_index("tensor") // 2
    dp_place = lax.axis_index("dp")
    small = dp_size == 8
    z_shifts = {k: [(i, (i + 2 * k) % 8) for i in range(8)] for k in (1, 2, 3)}
    y_pairs = [(i, i ^ 1) for i in range(dp_size)]

    one = jnp.where(dp_place < 0, 0.5, 1.0).astype(wide)

    def rounded(v):
        return (v * one).astype(bfloat)

    def swap_core(v):
        return lax.ppermute(v, "tensor", CORE_PAIRS)

    def swap_x(v):
        return lax.ppermute(v, "tensor", X_PAIRS)

    def my_half(v):
        return lax.dynamic_slice_in_dim(v, core * half, half, 0)

    def other_half(v):
        return lax.dynamic_slice_in_dim(v, (1 - core) * half, half, 0)

    def natural(mine, other):
        return jnp.where(
            core == 0, jnp.concatenate([mine, other], 0), jnp.concatenate([other, mine], 0)
        )

    def total_half(mine, other):
        both = mine + swap_core(other)
        return both + swap_x(both)

    def along_z(v, k):
        return lax.ppermute(v, "dp", z_shifts[k])

    def join_x(mine, other):
        return jnp.where(
            x_side == 0, jnp.concatenate([mine, other], 0), jnp.concatenate([other, mine], 0)
        )

    def sum_z(blocks):
        z = dp_place // 2
        split = blocks.reshape((4, 2) + blocks.shape[1:])
        total = lax.dynamic_index_in_dim(split, z, 0, False)
        for k in (1, 2, 3):
            total = total + along_z(lax.dynamic_index_in_dim(split, (z + k) % 4, 0, False), k)
        return total

    def sum_y(blocks):
        y = dp_place % 2
        kept = lax.dynamic_index_in_dim(blocks, y, 0, False)
        return kept + lax.ppermute(
            lax.dynamic_index_in_dim(blocks, 1 - y, 0, False), "dp", y_pairs
        )

    out_wide = out_grad.astype(wide)
    lane = jnp.arange(EXPERTS, dtype=jnp.int32)
    dense_gates = jnp.sum(
        jnp.where(routes[:, :, None] == lane[None, None, :], gates[:, :, None], 0.0), 1
    )
    quarter = half // 2
    og_mine, og_other = my_half(out_wide), other_half(out_wide)
    gates_mine, gates_other = my_half(dense_gates), other_half(dense_gates)
    shard = width // dp_size

    def my_quarter(v):
        return lax.dynamic_slice_in_dim(v, x_side * quarter, quarter, 0)

    if small:
        og_sent = jnp.concatenate(
            [my_quarter(og_mine), my_quarter(gates_mine).reshape(-1, width)], 0
        )
        og_z = {k: along_z(og_sent, k) for k in (1, 3, 2)}

    tokens_wide = tokens.astype(wide)
    normed1_low = norm_forward(tokens_wide, norm1_gain).astype(bfloat)
    query_proj = dot_nn(normed1_low, w_query)
    key_proj = dot_nn(normed1_low, w_key)
    value_low = (
        dot_nn(normed1_low, w_value).astype(bfloat).reshape(row_count, local_groups, HEAD_DIM)
    )
    cosine, sine_table = rope_tables(positions)

    def turn_query(proj_in):
        return rotate(proj_in.reshape(row_count, local_heads, HEAD_DIM), cosine, sine_table)

    def turn_key(proj_in):
        return rotate(proj_in.reshape(row_count, local_groups, HEAD_DIM), cosine, sine_table)

    query_rot, query_back = jax.vjp(turn_query, query_proj)
    key_rot, key_back = jax.vjp(turn_key, key_proj)
    query_low = query_rot.astype(bfloat).reshape(row_count, local_groups, per_group, HEAD_DIM)
    key_low = key_rot.astype(bfloat)
    key_index = jnp.arange(row_count, dtype=jnp.int32)

    def block_scores(block_num):
        row_start = block_num * block_rows
        query_block = query_low[row_start : row_start + block_rows]
        row_index = row_start + jnp.arange(block_rows, dtype=jnp.int32)
        place_gap = positions[row_start : row_start + block_rows][:, None] - positions[None, :]
        allowed = (row_index[:, None] >= key_index[None, :]) & (
            place_gap == row_index[:, None] - key_index[None, :]
        )
        raw_scores = (
            jnp.einsum("qgrd,kgd->grqk", query_block, key_low, preferred_element_type=wide)
            * scale_factor
        )
        return (jnp.where(allowed[None, None], raw_scores, -1e30), query_block)

    mixed_blocks = []
    log_totals = []
    for block_num in range(block_count):
        scores, query_block = block_scores(block_num)
        row_max = jnp.max(scores, -1, keepdims=True)
        exp_scores = jnp.exp(scores - row_max)
        row_total = jnp.sum(exp_scores, -1, keepdims=True)
        soft_low = (exp_scores / row_total).astype(bfloat)
        log_totals.append(row_max + jnp.log(row_total))
        mixed_blocks.append(
            jnp.einsum("grqk,kgd->qgrd", soft_low, value_low, preferred_element_type=wide)
        )
    mixed_low = (
        jnp.concatenate(mixed_blocks, 0).astype(bfloat).reshape(row_count, local_heads * HEAD_DIM)
    )
    ready = functools.partial(
        prepare,
        gain=norm2_gain,
        place=dp_place if small else jnp.zeros_like(dp_place),
        shard=shard if small else width // 8,
        half=half,
    )
    own_og, own_ogt = ready(og_mine, og_other, normed=False)
    own_gates = jnp.concatenate([gates_mine, gates_other], 0)
    if small:
        mixed_low, og_z[1] = together(mixed_low, og_z[1])
    attn_both = dot_nn(my_half(mixed_low), w_out) + swap_core(
        dot_nn(other_half(mixed_low), w_out)
    )
    attention = after(attn_both + swap_x(attn_both), own_og, own_ogt, own_gates)
    if small:
        attention, og_z[2] = together(attention, og_z[2])
    hidden = my_half(tokens_wide) + attention
    hidden_other = swap_core(hidden)
    weights = (w_gate, w_up, w_down)
    own_x, own_xt = ready(hidden, hidden_other, normed=True)
    ga, gu, n_part = own_experts(own_x, own_og, own_gates, *weights)
    if small:
        z_hidden = {2: along_z(my_quarter(hidden), 2)}
        og_x = {k: swap_x(og_z[k]) for k in (1, 2)}
        n_part, z_hidden[2], og_z[3], og_x[1], og_x[2] = together(
            n_part, z_hidden[2], og_z[3], og_x[1], og_x[2]
        )

    n_both = n_part[:half] + swap_core(n_part[half:])
    normed2_grad = n_both + swap_x(n_both)
    w_down2 = w_down.reshape(-1, width)
    e_both = dot_nn(ga[:half], w_down2) + swap_core(dot_nn(ga[half:], w_down2))
    waiting = [e_both]
    if small:
        def og_part(k):
            og_h = join_x(og_z[k][:quarter], og_x[k][:quarter])
            gates_h = join_x(og_z[k][quarter:], og_x[k][quarter:])
            og_h = jnp.concatenate([og_h, gates_h], 0)
            arrived = swap_core(og_h)
            prepared = ready(og_h, arrived, normed=False)
            both_gates = jnp.concatenate([gates_h, arrived[half:]], 0).reshape(-1, EXPERTS)
            return (*prepared, both_gates)

        og_parts = {k: og_part(k) for k in (1, 2)}
        z_hidden[1] = along_z(after(hidden, n_part), 1)
        waiting += [z_hidden[1], *og_parts[1], *og_parts[2]]
    normed2_grad, e_both, *waited = together(normed2_grad, *waiting)
    if small:
        z_hidden[1] = waited[0]
        og_parts = {1: waited[1:4], 2: waited[4:7]}
    hidden_part, gain2_grad = norm_backward(hidden, norm2_gain, normed2_grad)
    hidden_grad = my_half(out_wide) + hidden_part
    attn_grad = natural(hidden_grad.astype(bfloat), rounded(swap_core(hidden_grad)))
    if small:
        z_hidden[3] = along_z(after(hidden, normed2_grad), 3)
        og_x[3] = swap_x(after(og_z[3], normed2_grad))
        hidden_x = swap_x(after(z_hidden[2], normed2_grad))

    grad_w_out = jnp.einsum("tc,td->cd", mixed_low, attn_grad, preferred_element_type=wide)
    mixed_grad = dot_nt(attn_grad, w_out).astype(bfloat)
    mixed_grad = mixed_grad.reshape(row_count, local_groups, per_group, HEAD_DIM)
    key_grad = jnp.zeros((row_count, local_groups, HEAD_DIM), wide)
    value_grad = jnp.zeros((row_count, local_groups, HEAD_DIM), wide)
    query_grads = []
    for block_num in range(block_count):
        row_start = block_num * block_rows
        scores, query_block = block_scores(block_num)
        soft = jnp.exp(scores - log_totals[block_num])
        grad_block = mixed_grad[row_start : row_start + block_rows]
        prob_grad = jnp.einsum("qgrd,kgd->grqk", grad_block, value_low, preferred_element_type=wide)
        row_dot = jnp.sum(soft * prob_grad, -1, keepdims=True)
        score_grad = (soft * (prob_grad - row_dot)).astype(bfloat)
        query_grads.append(
            jnp.einsum("grqk,kgd->qgrd", score_grad, key_low, preferred_element_type=wide)
            * scale_factor
        )
        key_grad = (
            key_grad
            + jnp.einsum("grqk,qgrd->kgd", score_grad, query_block, preferred_element_type=wide)
            * scale_factor
        )
        value_grad = value_grad + jnp.einsum(
            "grqk,qgrd->kgd", soft.astype(bfloat), grad_block, preferred_element_type=wide
        )
    query_rot_grad = jnp.concatenate(query_grads, 0).reshape(row_count, local_heads, HEAD_DIM)
    (query_in,) = query_back(query_rot_grad)
    (key_in,) = key_back(key_grad)
    qkv_low = jnp.concatenate(
        [
            query_in.astype(bfloat),
            key_in.astype(bfloat),
            value_grad.astype(bfloat).reshape(row_count, local_groups * HEAD_DIM),
        ],
        1,
    )
    w_qkv = jnp.concatenate([w_query, w_key, w_value], 1)
    if small:
        qkv_low, og_x[3], hidden_x, z_hidden[3] = together(
            qkv_low, og_x[3], hidden_x, z_hidden[3]
        )
    t_both = dot_nt(my_half(qkv_low), w_qkv) + swap_core(dot_nt(other_half(qkv_low), w_qkv))
    normed1_grad = t_both + swap_x(t_both)
    tokens_mine = my_half(tokens_wide)
    tokens_part, gain1_grad = norm_backward(tokens_mine, norm1_gain, normed1_grad)
    tokens_half = hidden_grad + tokens_part
    expert_total = e_both + swap_x(after(e_both, t_both))
    block_mine = hidden + expert_total

    grad_w_qkv = jnp.einsum("td,tc->dc", normed1_low, qkv_low, preferred_element_type=wide)
    gain2_grad = gain2_grad + swap_core(gain2_grad)
    joined = jnp.concatenate(
        [
            grad_w_qkv.reshape(dp_size, grad_w_qkv.shape[1], shard),
            grad_w_out.reshape(w_out.shape[0], dp_size, shard).transpose(1, 0, 2),
            jnp.broadcast_to(gain2_grad.reshape(dp_size, 1, shard), (dp_size, 8, shard)),
        ],
        1,
    )
    gain1_grad = (gain1_grad + swap_core(gain1_grad)).reshape(dp_size, -1)

    if small:
        og_parts[3] = og_part(3)
        hidden_parts = {}
        for k in (1, 2, 3):
            hidden_h = z_hidden[k] if k != 2 else join_x(z_hidden[2], hidden_x)
            hidden_parts[k] = ready(hidden_h, swap_core(hidden_h), normed=True)
        shifts = (1, 2, 3)
        xs = [hidden_parts[k][0] for k in shifts]
        xs = list(lax.optimization_barrier((*xs, t_both))[:3])
        pieces = []
        first = 0
        joined = sum_z(joined)
        for number, count in enumerate(CHUNK_SIZES):
            if number == 1:
                *xs, tokens_half, joined = together(*xs, tokens_half, joined)
                joined = sum_y(joined)
                gain1 = sum_z(gain1_grad)
            if number == 2:
                *xs, block_mine, gain1, pieces[0] = together(*xs, block_mine, gain1, pieces[0])
                gain1 = sum_y(gain1)
            if number == 3:
                *xs, joined, gain1, pieces[1] = together(*xs, joined, gain1, pieces[1])
            keep, send = expert_grads(
                first,
                count,
                xs,
                [og_parts[k][0] for k in shifts],
                [og_parts[k][2] for k in shifts],
                [hidden_parts[k][1] for k in shifts],
                [og_parts[k][1] for k in shifts],
                own_xt,
                own_ogt,
                ga,
                gu,
                weights,
            )
            first += count
            pieces.append(keep + lax.ppermute(send, "dp", y_pairs))
        block_out = place_halves(block_mine, swap_core(block_mine), core)
        tokens_grad = place_halves(tokens_half, swap_core(tokens_half), core)
        *pieces, block_out, tokens_grad = together(*pieces, block_out, tokens_grad)
        grad_w_gate, grad_w_up, grad_w_down = (
            jnp.concatenate([c[:, i] for c in pieces], 0) for i in range(3)
        )
    else:
        joined = lax.psum_scatter(joined, "dp", scatter_dimension=0, tiled=True)[0]
        gain1 = lax.psum_scatter(gain1_grad, "dp", scatter_dimension=0, tiled=True)[0]
        block_out = place_halves(block_mine, swap_core(block_mine), core)
        tokens_grad = place_halves(tokens_half, swap_core(tokens_half), core)
        ga = ga.reshape(row_count, EXPERTS, -1)
        gu = gu.reshape(row_count, EXPERTS, 2, -1)
        grad_w_gate = jnp.einsum("td,tef->edf", own_x, gu[:, :, 0], preferred_element_type=wide)
        grad_w_up = jnp.einsum("td,tef->edf", own_x, gu[:, :, 1], preferred_element_type=wide)
        grad_w_down = jnp.einsum("tef,td->efd", ga, own_og, preferred_element_type=wide)
        grad_w_gate = lax.psum_scatter(grad_w_gate, "dp", scatter_dimension=1, tiled=True)
        grad_w_up = lax.psum_scatter(grad_w_up, "dp", scatter_dimension=1, tiled=True)
        grad_w_down = lax.psum_scatter(grad_w_down, "dp", scatter_dimension=2, tiled=True)

    qkv_rows = grad_w_qkv.shape[1]
    grad_w_qkv = joined[:qkv_rows].reshape(shard, -1)
    grad_w_out = joined[qkv_rows : qkv_rows + w_out.shape[0]]
    gain2 = joined[-8]
    query_cols, key_cols = w_query.shape[1], w_key.shape[1]
    return (
        block_out,
        tokens_grad,
        gain1,
        grad_w_qkv[:, :query_cols],
        grad_w_qkv[:, query_cols : query_cols + key_cols],
        grad_w_qkv[:, query_cols + key_cols :],
        grad_w_out,
        gain2,
        grad_w_gate,
        grad_w_up,
        grad_w_down,
    )


def solution(mesh):
    placed = (
        P("dp", None),
        P("dp"),
        P("dp", None),
        P("dp", None),
        P(),
        P(None, "tensor"),
        P(None, "tensor"),
        P(None, "tensor"),
        P("tensor", None),
        P(),
        P(None, None, "tensor"),
        P(None, None, "tensor"),
        P(None, "tensor", None),
        P("dp", None),
    )
    return jax.shard_map(
        functools.partial(per_device, mesh.shape["dp"]),
        mesh=mesh,
        in_specs=placed,
        out_specs=(
            P("dp", None),
            P("dp", None),
            P("dp"),
            P("dp", "tensor"),
            P("dp", "tensor"),
            P("dp", "tensor"),
            P("tensor", "dp"),
            P("dp"),
            P(None, "dp", "tensor"),
            P(None, "dp", "tensor"),
            P(None, "tensor", "dp"),
        ),
        check_vma=False,
    )
```

time: 944 us -> 635 us (0.67)
  waiting for transfers between devices: 300 us -> 101 us
  starting transfers between devices: 102 us -> 40.6 us
  other arithmetic: 131 us -> 75.4 us
  Pallas kernels: 246 us -> 275 us
  local copies, waits for them, and re-layouts: 93 us -> 70.1 us
    ppermute x46 -> x18, waiting for transfers between devices: 260 us -> 21.9 us  [the longest x4 19.5 us: per_device(): pieces.append(keep + lax.ppermute(send, 'dp', y_pairs))]
    ppermute x46 -> x18, starting transfers between devices: 93.2 us -> 29.1 us  [the longest x12 22.2 us: along_z(): return lax.ppermute(v, 'dp', z_shifts[k])]
    ppermute x5 -> x8, waiting for transfers between devices: 36.2 us -> 74.8 us  [swap_x(): return lax.ppermute(v, 'tensor', X_PAIRS)]
    pallas_call x6 -> x15, Pallas kernels: 246 us -> 275 us  [the longest x4 158 us: expert_grads(): pl.pallas_call(functools.partial(grads_body, first, len(x)), grid=(count...]
    convert_element_type x4 -> x0, local copies, waits for them, and re-layouts: 21.5 us -> none  [the longest x3 20 us: rounded(): return (v * one).astype(bfloat)]
    unnamed x267 -> x149, local copies, waits for them, and re-layouts: 46.6 us -> 26.1 us
    convert_element_type x4 -> x1, other arithmetic: 19.2 us -> 1.83 us  [rounded(): return (v * one).astype(bfloat)]
    select_n x7, other arithmetic: 21 us -> 5.01 us  [join_x(): jnp.where(x_side == 0, jnp.concatenate([mine, other], 0), jnp.concatenate...]
  transfers between devices with their start and end apart: 63 -> 42, of which waited for: 22 -> 9; matrix products, arithmetic and copies ran while one was open for 25% -> 25% of each run, Pallas kernels for 26% -> 44%
where the time goes in v2:
time: 635 us; the launch traced here: 624 us
  Pallas kernels  275 us (43%)
  waiting for transfers between devices  101 us (16%)
  other arithmetic  75.4 us (12%)
  local copies, waits for them, and re-layouts  70.1 us (11%)
  matrix products  58.7 us (9%)
  starting transfers between devices  40.6 us (6%)
    pallas_call x4, Pallas kernels, expert_grads(): pl.pallas_call(functools.partial(grads_body, first, len(x)), grid=(count...  158 us
    ppermute x8, waiting for transfers between devices, swap_x(): return lax.ppermute(v, 'tensor', X_PAIRS)  74.8 us
    pallas_call x1, Pallas kernels, own_experts(): pl.pallas_call(own_body, grid=(experts // 2,), in_specs=[whole(x), whole(...  66.4 us
    pallas_call x8, Pallas kernels, prepare(): pl.pallas_call(functools.partial(prepare_body, normed), grid_spec=pltpu.P...  40.3 us
    unnamed x149, local copies, waits for them, and re-layouts  26.1 us
    dot_general x7, matrix products, dot_nn(): return jnp.dot(a, b, preferred_element_type=wide)  22.4 us
    ppermute x12, starting transfers between devices, along_z(): return lax.ppermute(v, 'dp', z_shifts[k])  22.2 us
    ppermute x4, waiting for transfers between devices, per_device(): pieces.append(keep + lax.ppermute(send, 'dp', y_pairs))  19.5 us
  transfers between devices with their start and end apart: 42, of which 9 were waited for; matrix products, arithmetic and copies ran while one was open for 25% of the time, Pallas kernels for 44%

profile of v2, /device:TPU:0, one launch (start us, length us, event | category | flops | bytes accessed | tf_op | source)
XLA Modules:
  0.0 624.0 jit_solution(6417733086569091060)
XLA Ops:
  31.5 5.4 fusion.44
  50.1 4.8 constant_dynamic-slice_fusion.9
  54.9 4.9 prepare.8
  59.9 31.7 %collective-permute-done.2 = f32[512,1024]{1,0:T(8,128)} collective-permute-done((f32[512,1024]{1,0:T(8,128)}, f32[512,1024]{1,0:T(8,128)}, u32[]{:S(2)}, u32[]{:S(2)}) %collective-permute-start.2) | collective-permute-done | bytes 2097184 | tf_op jit(solution)/shard_map/ppermute | solution.py:358
  103.6 5.2 prepare.9
  110.4 66.4 %own_experts.1 = (bf16[1024,4096]{1,0:T(8,128)(2,1)}, bf16[1024,8192]{1,0:T(8,128)(2,1)}, f32[1024,1024]{1,0:T(8,128)S(1)}) custom-call(bf16[1024,1024]{1,0:T(8,128)(2,1)S(1)} %copy-done.5, bf16[1024,1024]{1,0:T(8,128)(2,1)S(1)} %copy-done.4, f32[1024,32]{1,0:T(8,128)S(1)} %copy.87.g_ref, bf16[32,1024,128]{2,1,0:T(8,128)(2,1)} %refs_19_.7, ...), custom_call_target="tpu_custom_call" | custom-call | flops 1048576 | bytes 1048576 | tf_op jit(solution)/shard_map/own_experts/pallas_call | solution.py:119
  179.4 10.5 %fusion.16 = f32[512,1024]{1,0:T(8,128)} fusion(bf16[4096,1024]{1,0:T(8,128)(2,1)} %bitcast.189, bf16[1024,4096]{1,0:T(8,128)(2,1)} %get-tuple-element.102.refs_17_), kind=kOutput, calls=%fused_computation.26 | convolution fusion | flops 4294967296 | bytes 14680064 | tf_op jit(solution)/shard_map/dot_general | solution.py:27
  211.7 7.0 %fusion.24 = f32[512,1024]{1,0:T(8,128)} fusion(f32[512,1024]{1,0:T(8,128)} %collective-permute-done.11, bf16[4096,1024]{1,0:T(8,128)(2,1)S(1)} %bitcast.192, bf16[1024,4096]{1,0:T(8,128)(2,1)S(1)} %copy-done.8), kind=kOutput, calls=%fused_computation.69 | convolution fusion | flops 4295491584 | bytes 16777216 | tf_op jit(solution)/shard_map/dot_general | solution.py:27
  222.9 4.9 prepare.10
  227.8 5.0 prepare.11
  232.8 24.9 %collective-permute-done.10 = f32[512,1024]{1,0:T(8,128)} collective-permute-done((f32[512,1024]{1,0:T(8,128)}, f32[512,1024]{1,0:T(8,128)}, u32[]{:S(2)}, u32[]{:S(2)}) %collective-permute-start.10) | collective-permute-done | bytes 2097184 | tf_op jit(solution)/shard_map/ppermute | solution.py:358
  277.9 5.3 fusion.3
  301.3 18.2 %collective-permute-done.18 = f32[256,1024]{1,0:T(8,128)} collective-permute-done((f32[256,1024]{1,0:T(8,128)}, f32[256,1024]{1,0:T(8,128)}, u32[]{:S(2)}, u32[]{:S(2)}) %collective-permute-start.18) | collective-permute-done | bytes 1048608 | tf_op jit(solution)/shard_map/ppermute | solution.py:358
  357.1 5.1 prepare.12
  362.1 5.1 prepare.13
  367.2 5.1 prepare.14
  374.2 5.0 prepare.15
  379.1 39.2 %expert_grads.4 = (f32[8,3,128,128]{3,2,1,0:T(8,128)}, f32[8,3,128,128]{3,2,1,0:T(8,128)}) custom-call(bf16[1024,1024]{1,0:T(8,128)(2,1)} %get-tuple-element.158.refs_0_, bf16[1024,1024]{1,0:T(8,128)(2,1)} %get-tuple-element.159.refs_1_, bf16[1024,1024]{1,0:T(8,128)(2,1)} %get-tuple-element.160.refs_2_, bf16[1024,1024]{1,0:T(8,128)(2,1)} %get-tuple-element.131.refs_3_, ...), custom_call_target="tpu_custom_call" | custom-call | flops 1048576 | bytes 1048576 | tf_op jit(solution)/shard_map/expert_grads/pallas_call | solution.py:204
  433.1 39.5 %expert_grads.5 = (f32[8,3,128,128]{3,2,1,0:T(8,128)}, f32[8,3,128,128]{3,2,1,0:T(8,128)}) custom-call(bf16[1024,1024]{1,0:T(8,128)(2,1)} %get-tuple-element.158.refs_0_, bf16[1024,1024]{1,0:T(8,128)(2,1)} %get-tuple-element.159.refs_1_, bf16[1024,1024]{1,0:T(8,128)(2,1)} %get-tuple-element.160.refs_2_, bf16[1024,1024]{1,0:T(8,128)(2,1)} %get-tuple-element.131.refs_3_, ...), custom_call_target="tpu_custom_call" | custom-call | flops 1048576 | bytes 1048576 | tf_op jit(solution)/shard_map/expert_grads/pallas_call | solution.py:204
  490.2 39.7 %expert_grads.6 = (f32[8,3,128,128]{3,2,1,0:T(8,128)}, f32[8,3,128,128]{3,2,1,0:T(8,128)}) custom-call(bf16[1024,1024]{1,0:T(8,128)(2,1)} %get-tuple-element.158.refs_0_, bf16[1024,1024]{1,0:T(8,128)(2,1)} %get-tuple-element.159.refs_1_, bf16[1024,1024]{1,0:T(8,128)(2,1)} %get-tuple-element.160.refs_2_, bf16[1024,1024]{1,0:T(8,128)(2,1)} %get-tuple-element.131.refs_3_, ...), custom_call_target="tpu_custom_call" | custom-call | flops 1048576 | bytes 1048576 | tf_op jit(solution)/shard_map/expert_grads/pallas_call | solution.py:204
  537.3 39.7 %expert_grads.7 = (f32[8,3,128,128]{3,2,1,0:T(8,128)}, f32[8,3,128,128]{3,2,1,0:T(8,128)}) custom-call(bf16[1024,1024]{1,0:T(8,128)(2,1)} %get-tuple-element.158.refs_0_, bf16[1024,1024]{1,0:T(8,128)(2,1)} %get-tuple-element.159.refs_1_, bf16[1024,1024]{1,0:T(8,128)(2,1)} %get-tuple-element.160.refs_2_, bf16[1024,1024]{1,0:T(8,128)(2,1)} %get-tuple-element.131.refs_3_, ...), custom_call_target="tpu_custom_call" | custom-call | flops 1048576 | bytes 1048576 | tf_op jit(solution)/shard_map/expert_grads/pallas_call | solution.py:204
  583.9 5.2 place_halves.3
  589.1 5.4 place_halves.2
  594.5 19.4 %collective-permute-done.39 = f32[8,3,128,128]{3,2,1,0:T(8,128)} collective-permute-done((f32[8,3,128,128]{3,2,1,0:T(8,128)}, f32[8,3,128,128]{3,2,1,0:T(8,128)}, u32[]{:S(2)}, u32[]{:S(2)}) %collective-permute-start.39) | collective-permute-done | bytes 1572896 | tf_op jit(solution)/shard_map/ppermute | solution.py:625
  (374 shorter events, 219.1 us)
Async XLA Ops:
  43.6 48.0 %collective-permute-start.2 = (f32[512,1024]{1,0:T(8,128)}, f32[512,1024]{1,0:T(8,128)}, u32[]{:S(2)}, u32[]{:S(2)}) collective-permute-start(f32[512,1024]{1,0:T(8,128)} %convolution_add_fusion.1), channel_id=1, source_target_pairs={{0,2},{1,3},{2,0},{3,1},{4,6},{5,7},{6,4},{7,5},{8,10},{9,11},{10,... | collective-permute-start | bytes 6291464 | tf_op jit(solution)/shard_map/ppermute | solution.py:358
  45.0 50.0 %collective-permute-start.3 = (f32[264,1024]{1,0:T(8,128)}, f32[264,1024]{1,0:T(8,128)}, u32[]{:S(2)}, u32[]{:S(2)}) collective-permute-start(f32[264,1024]{1,0:T(8,128)} %pad_maximum_fusion.7), channel_id=1, source_target_pairs={{0,16},{4,20},{8,24},{12,28},{16,0},{20,4},{24,8},{28,12},{1,17},{... | collective-permute-start | bytes 3244040 | tf_op jit(solution)/shard_map/ppermute | solution.py:376
  96.7 80.0 %collective-permute-start.6 = (f32[264,1024]{1,0:T(8,128)}, f32[264,1024]{1,0:T(8,128)}, u32[]{:S(2)}, u32[]{:S(2)}) collective-permute-start(f32[264,1024]{1,0:T(8,128)} %pad_maximum_fusion.7), channel_id=1, source_target_pairs={{0,24},{4,28},{8,0},{12,4},{16,8},{20,12},{24,16},{28,20},{1,25},{... | collective-permute-start | bytes 3244040 | tf_op jit(solution)/shard_map/ppermute | solution.py:376
  99.0 77.7 %collective-permute-start.7 = (f32[264,1024]{1,0:T(8,128)}, f32[264,1024]{1,0:T(8,128)}, u32[]{:S(2)}, u32[]{:S(2)}) collective-permute-start(f32[264,1024]{1,0:T(8,128)} %collective-permute-done), channel_id=1, source_target_pairs={{0,2},{1,3},{2,0},{3,1},{4,6},{5,7},{6,4},{7,5},{8,10},{9,11},{10,... | collective-permute-start | bytes 3244040 | tf_op jit(solution)/shard_map/ppermute | solution.py:358
  99.6 77.2 %collective-permute-start.8 = (f32[264,1024]{1,0:T(8,128)}, f32[264,1024]{1,0:T(8,128)}, u32[]{:S(2)}, u32[]{:S(2)}) collective-permute-start(f32[264,1024]{1,0:T(8,128)} %collective-permute-done.3), channel_id=1, source_target_pairs={{0,2},{1,3},{2,0},{3,1},{4,6},{5,7},{6,4},{7,5},{8,10},{9,11},{10,... | collective-permute-start | bytes 3244040 | tf_op jit(solution)/shard_map/ppermute | solution.py:358
  103.3 73.4 %collective-permute-start.5 = (f32[256,1024]{1,0:T(8,128)}, f32[256,1024]{1,0:T(8,128)}, u32[]{:S(2)}, u32[]{:S(2)}) collective-permute-start(f32[256,1024]{1,0:T(8,128)} %constant_dynamic-slice_fusion.6), channel_id=1, source_target_pairs={{0,16},{4,20},{8,24},{12,28},{16,0},{20,4},{24,8},{28,12},{1,17},{... | collective-permute-start | bytes 3145736 | tf_op jit(solution)/shard_map/ppermute | solution.py:376
  198.9 61.5 %collective-permute-start.12 = (f32[512,1024]{1,0:T(8,128)}, f32[512,1024]{1,0:T(8,128)}, u32[]{:S(2)}, u32[]{:S(2)}) collective-permute-start(f32[512,1024]{1,0:T(8,128)} %get-tuple-element.117.mine_ref), channel_id=1, source_target_pairs={{0,8},{4,12},{8,16},{12,20},{16,24},{20,28},{24,0},{28,4},{1,9},{5... | collective-permute-start | bytes 6291464 | tf_op jit(solution)/shard_map/ppermute | solution.py:376
  210.2 47.6 %collective-permute-start.10 = (f32[512,1024]{1,0:T(8,128)}, f32[512,1024]{1,0:T(8,128)}, u32[]{:S(2)}, u32[]{:S(2)}) collective-permute-start(f32[512,1024]{1,0:T(8,128)} %slice_add_fusion), channel_id=1, source_target_pairs={{0,2},{1,3},{2,0},{3,1},{4,6},{5,7},{6,4},{7,5},{8,10},{9,11},{10,... | collective-permute-start | bytes 6291464 | tf_op jit(solution)/shard_map/ppermute | solution.py:358
  270.4 49.1 %collective-permute-start.17 = (f32[264,1024]{1,0:T(8,128)}, f32[264,1024]{1,0:T(8,128)}, u32[]{:S(2)}, u32[]{:S(2)}) collective-permute-start(f32[264,1024]{1,0:T(8,128)} %collective-permute-done.6), channel_id=1, source_target_pairs={{0,2},{1,3},{2,0},{3,1},{4,6},{5,7},{6,4},{7,5},{8,10},{9,11},{10,... | collective-permute-start | bytes 3244040 | tf_op jit(solution)/shard_map/ppermute | solution.py:358
  272.0 47.5 %collective-permute-start.18 = (f32[256,1024]{1,0:T(8,128)}, f32[256,1024]{1,0:T(8,128)}, u32[]{:S(2)}, u32[]{:S(2)}) collective-permute-start(f32[256,1024]{1,0:T(8,128)} %collective-permute-done.5), channel_id=1, source_target_pairs={{0,2},{1,3},{2,0},{3,1},{4,6},{5,7},{6,4},{7,5},{8,10},{9,11},{10,... | collective-permute-start | bytes 3145736 | tf_op jit(solution)/shard_map/ppermute | solution.py:358
  272.5 48.0 %collective-permute-start.19 = (f32[512,1024]{1,0:T(8,128)}, f32[512,1024]{1,0:T(8,128)}, u32[]{:S(2)}, u32[]{:S(2)}) collective-permute-start(f32[512,1024]{1,0:T(8,128)} %get-tuple-element.117.mine_ref), channel_id=1, source_target_pairs={{0,24},{4,28},{8,0},{12,4},{16,8},{20,12},{24,16},{28,20},{1,25},{... | collective-permute-start | bytes 6291464 | tf_op jit(solution)/shard_map/ppermute | solution.py:376
  333.8 38.5 %collective-permute-start.33 = (f32[528,1024]{1,0:T(8,128)}, f32[528,1024]{1,0:T(8,128)}, u32[]{:S(2)}, u32[]{:S(2)}) collective-permute-start(f32[528,1024]{1,0:T(8,128)} %pad_maximum_fusion.3.mine_ref), channel_id=1, source_target_pairs={{0,1},{1,0},{2,3},{3,2},{4,5},{5,4},{6,7},{7,6},{8,9},{9,8},{10,11... | collective-permute-start | bytes 6488072 | tf_op jit(solution)/shard_map/ppermute | solution.py:355
  337.3 88.2 %collective-permute-start.23 = (f32[512,1024]{1,0:T(8,128)S(1)}, f32[512,1024]{1,0:T(8,128)}, u32[]{:S(2)}, u32[]{:S(2)}) collective-permute-start(f32[512,1024]{1,0:T(8,128)S(1)} %convolution_add_fusion), channel_id=1, source_target_pairs={{0,2},{1,3},{2,0},{3,1},{4,6},{5,7},{6,4},{7,5},{8,10},{9,11},{10,... | collective-permute-start | bytes 6291464 | tf_op jit(solution)/shard_map/ppermute | solution.py:358
  352.4 70.1 %collective-permute-start.27 = (f32[2,776,128]{2,1,0:T(8,128)}, f32[2,776,128]{2,1,0:T(8,128)S(1)}, u32[]{:S(2)}, u32[]{:S(2)}) collective-permute-start(f32[2,776,128]{2,1,0:T(8,128)} %get-tuple-element.185), channel_id=1, source_target_pairs={{0,24},{4,28},{8,0},{12,4},{16,8},{20,12},{24,16},{28,20},{1,25},{... | collective-permute-start | bytes 2383880 | tf_op jit(solution)/shard_map/ppermute | solution.py:376
  356.4 67.3 %collective-permute-start.26 = (f32[2,776,128]{2,1,0:T(8,128)}, f32[2,776,128]{2,1,0:T(8,128)}, u32[]{:S(2)}, u32[]{:S(2)}) collective-permute-start(f32[2,776,128]{2,1,0:T(8,128)} %get-tuple-element.186), channel_id=1, source_target_pairs={{0,16},{4,20},{8,24},{12,28},{16,0},{20,4},{24,8},{28,12},{1,17},{... | collective-permute-start | bytes 2383880 | tf_op jit(solution)/shard_map/ppermute | solution.py:376
  356.4 67.3 %collective-permute-start.25 = (f32[2,776,128]{2,1,0:T(8,128)}, f32[2,776,128]{2,1,0:T(8,128)}, u32[]{:S(2)}, u32[]{:S(2)}) collective-permute-start(f32[2,776,128]{2,1,0:T(8,128)} %get-tuple-element.184), channel_id=1, source_target_pairs={{0,8},{4,12},{8,16},{12,20},{16,24},{20,28},{24,0},{28,4},{1,9},{5... | collective-permute-start | bytes 2383880 | tf_op jit(solution)/shard_map/ppermute | solution.py:376
  421.0 54.8 %collective-permute-start.34 = (f32[8,3,128,128]{3,2,0,1:T(8,128)}, f32[8,3,128,128]{3,2,0,1:T(8,128)}, u32[]{:S(2)}, u32[]{:S(2)}) collective-permute-start(f32[8,3,128,128]{3,2,0,1:T(8,128)} %copy.95), channel_id=1, source_target_pairs={{0,4},{4,0},{8,12},{12,8},{16,20},{20,16},{24,28},{28,24},{1,5},{5... | collective-permute-start | bytes 4718600 | tf_op jit(solution)/shard_map/ppermute | solution.py:625
  422.5 61.0 %collective-permute-start.28 = (f32[512,1024]{1,0:T(8,128)}, f32[512,1024]{1,0:T(8,128)}, u32[]{:S(2)}, u32[]{:S(2)}) collective-permute-start(f32[512,1024]{1,0:T(8,128)} %fusion.24), channel_id=1, source_target_pairs={{0,2},{1,3},{2,0},{3,1},{4,6},{5,7},{6,4},{7,5},{8,10},{9,11},{10,... | collective-permute-start | bytes 6291464 | tf_op jit(solution)/shard_map/ppermute | solution.py:358
  474.3 60.2 %collective-permute-start.37 = (f32[8,3,128,128]{3,2,0,1:T(8,128)S(1)}, f32[8,3,128,128]{3,2,0,1:T(8,128)}, u32[]{:S(2)}, u32[]{:S(2)}) collective-permute-start(f32[8,3,128,128]{3,2,0,1:T(8,128)S(1)} %copy.97), channel_id=1, source_target_pairs={{0,4},{4,0},{8,12},{12,8},{16,20},{20,16},{24,28},{28,24},{1,5},{5... | collective-permute-start | bytes 4718600 | tf_op jit(solution)/shard_map/ppermute | solution.py:625
  478.7 55.8 %collective-permute-start.35 = (f32[776,128]{1,0:T(8,128)S(1)}, f32[776,128]{1,0:T(8,128)S(1)}, u32[]{:S(2)}, u32[]{:S(2)}) collective-permute-start(f32[776,128]{1,0:T(8,128)S(1)} %dynamic-slice_bitcast_fusion.3), channel_id=1, source_target_pairs={{0,4},{4,0},{8,12},{12,8},{16,20},{20,16},{24,28},{28,24},{1,5},{5... | collective-permute-start | bytes 1191944 | tf_op jit(solution)/shard_map/ppermute | solution.py:394
  489.1 44.6 %collective-permute-start.36 = (f32[128]{0:T(128)S(1)}, f32[128]{0:T(128)S(1)}, u32[]{:S(2)}, u32[]{:S(2)}) collective-permute-start(f32[128]{0:T(128)S(1)} %fusion.74), channel_id=1, source_target_pairs={{0,4},{4,0},{8,12},{12,8},{16,20},{20,16},{24,28},{28,24},{1,5},{5... | collective-permute-start | bytes 1544 | tf_op jit(solution)/shard_map/ppermute | solution.py:394
  490.2 93.7 %collective-permute-start.41 = (f32[512,1024]{1,0:T(8,128)}, f32[512,1024]{1,0:T(8,128)}, u32[]{:S(2)}, u32[]{:S(2)}) collective-permute-start(f32[512,1024]{1,0:T(8,128)} %subtract_add_fusion.mine_ref), channel_id=1, source_target_pairs={{0,1},{1,0},{2,3},{3,2},{4,5},{5,4},{6,7},{7,6},{8,9},{9,8},{10,11... | collective-permute-start | bytes 6291464 | tf_op jit(solution)/shard_map/ppermute | solution.py:355
  532.7 48.0 %collective-permute-start.38 = (f32[8,3,128,128]{3,2,0,1:T(8,128)}, f32[8,3,128,128]{3,2,0,1:T(8,128)}, u32[]{:S(2)}, u32[]{:S(2)}) collective-permute-start(f32[8,3,128,128]{3,2,0,1:T(8,128)} %copy.99), channel_id=1, source_target_pairs={{0,4},{4,0},{8,12},{12,8},{16,20},{20,16},{24,28},{28,24},{1,5},{5... | collective-permute-start | bytes 4718600 | tf_op jit(solution)/shard_map/ppermute | solution.py:625
  533.7 55.4 %collective-permute-start.40 = (f32[512,1024]{1,0:T(8,128)S(1)}, f32[512,1024]{1,0:T(8,128)}, u32[]{:S(2)}, u32[]{:S(2)}) collective-permute-start(f32[512,1024]{1,0:T(8,128)S(1)} %add_add_fusion.mine_ref), channel_id=1, source_target_pairs={{0,1},{1,0},{2,3},{3,2},{4,5},{5,4},{6,7},{7,6},{8,9},{9,8},{10,11... | collective-permute-start | bytes 6291464 | tf_op jit(solution)/shard_map/ppermute | solution.py:355
  (91 other events, 748.2 us)

commit v3 on v2

--- a/solution.py
+++ b/solution.py
@@ -12,7 +12,7 @@
 TOP = 8
 EPS = 1e-06
 ROPE_BASE = 10000.0
-CHUNK_SIZES = (8, 8, 8, 8)
+CHUNK_SIZES = (8, 10, 8, 6)
 
 bfloat = jnp.bfloat16
 wide = jnp.float32
@@ -57,9 +57,8 @@
     return values_in * cosine[:, None, :] + turned * sine_table[:, None, :]
 
 
-def expert_parts(x, og, gate_cols, w_pair, wd2):
-    hidden = wd2.shape[0] // 2
-    back = dot_nt(og, wd2)
+def expert_parts(x, back, gate_cols, w_pair):
+    hidden = back.shape[1] // 2
     out = []
     for j in range(2):
         both = dot_nn(x, w_pair[j])
@@ -68,7 +67,7 @@
         sig = 0.5 * jnp.tanh(0.5 * gate) + 0.5
         act = gate * sig
         slope = sig + act * (1.0 - sig)
-        weighted = back[:, j * hidden : (j + 1) * hidden] * col
+        weighted = back[:, j * hidden : (j + 1) * hidden].astype(wide) * col
         out.append(
             (
                 (act * up * col).astype(bfloat),
@@ -86,33 +85,94 @@
     ]
 
 
-def own_body(x_ref, og_ref, g_ref, wg_ref, wu_ref, wd_ref, ga_ref, gu_ref, n_ref):
+def own_body(x_ref, back_ref, g_ref, wg_ref, wu_ref, ga_ref, gu_ref, *n_refs):
     pair = pl.program_id(0)
     hidden = wg_ref.shape[2]
 
     @pl.when(pair == 0)
     def _():
-        n_ref[...] = jnp.zeros_like(n_ref)
+        for n_ref in n_refs:
+            n_ref[...] = jnp.zeros_like(n_ref)
 
     w_pair = [jnp.concatenate([wg_ref[j], wu_ref[j]], axis=1) for j in range(2)]
-    wd2 = wd_ref[...].reshape(2 * hidden, wd_ref.shape[2])
     cols = gate_columns(g_ref[...], 2 * pair)
-    parts = expert_parts(x_ref[...], og_ref[...], cols, w_pair, wd2)
-    total = n_ref[...]
+    parts = expert_parts(x_ref[...], back_ref[...], cols, w_pair)
+    half = n_refs[0].shape[0]
+    totals = [n_ref[...] for n_ref in n_refs]
     for j in range(2):
         ga, gg, ug = parts[j]
         ga_ref[:, j * hidden : (j + 1) * hidden] = ga
         gu = jnp.concatenate([gg, ug], axis=1)
         gu_ref[:, 2 * j * hidden : 2 * (j + 1) * hidden] = gu
-        total = total + dot_nt(gu, w_pair[j])
-    n_ref[...] = total
+        for i in range(2):
+            totals[i] = totals[i] + dot_nt(gu[i * half : (i + 1) * half], w_pair[j])
+    for n_ref, total in zip(n_refs, totals):
+        n_ref[...] = total
+
+
+def back_body(og_ref, wd_ref, out_ref):
+    for i in range(out_ref.shape[0]):
+        wd2 = wd_ref[2 * i : 2 * i + 2].reshape(-1, wd_ref.shape[2])
+        out_ref[i] = dot_nt(og_ref[...], wd2).astype(bfloat)
+
+
+def back_through_down(og, w_down):
+    rows, width = og.shape
+    experts, hidden, _ = w_down.shape
+    return pl.pallas_call(
+        back_body,
+        grid=(experts // 4,),
+        in_specs=[whole(og), pl.BlockSpec((4, hidden, width), lambda p: (p, 0, 0))],
+        out_specs=pl.BlockSpec((2, rows, 2 * hidden), lambda p: (p, 0, 0)),
+        out_shape=jax.ShapeDtypeStruct((experts // 2, rows, 2 * hidden), bfloat),
+        compiler_params=pltpu.CompilerParams(
+            dimension_semantics=("arbitrary",), vmem_limit_bytes=58 * 2**20
+        ),
+        cost_estimate=BRIEF,
+        name="back_through_down",
+    )(og, w_down)
+
+
+def down_body(ga_ref, wd_ref, *out_refs):
+    @pl.when(pl.program_id(0) == 0)
+    def _():
+        for out_ref in out_refs:
+            out_ref[...] = jnp.zeros_like(out_ref)
+
+    wd = wd_ref[...].reshape(-1, wd_ref.shape[2])
+    half = out_refs[0].shape[0]
+    for i, out_ref in enumerate(out_refs):
+        rows = slice(i * half, (i + 1) * half)
+        ga = jnp.concatenate([ga_ref[n, rows, :] for n in range(ga_ref.shape[0])], axis=1)
+        out_ref[...] += dot_nn(ga, wd)
+
+
+def down_products(ga, w_down):
+    rows = ga.shape[1]
+    experts, hidden, width = w_down.shape
+    out = jax.ShapeDtypeStruct((rows // 2, width), wide)
+    return pl.pallas_call(
+        down_body,
+        grid=(experts // 4,),
+        in_specs=[
+            pl.BlockSpec((2, rows, 2 * hidden), lambda p: (p, 0, 0)),
+            pl.BlockSpec((4, hidden, width), lambda p: (p, 0, 0)),
+        ],
+        out_specs=[pl.BlockSpec((rows // 2, width), lambda p: (0, 0))] * 2,
+        out_shape=[out, out],
+        compiler_params=pltpu.CompilerParams(
+            dimension_semantics=("arbitrary",), vmem_limit_bytes=58 * 2**20
+        ),
+        cost_estimate=BRIEF,
+        name="down_products",
+    )(ga, w_down)
 
 
 def whole(a):
     return pl.BlockSpec(a.shape, lambda *_: (0,) * a.ndim, pipeline_mode=pl.Buffered(1))
 
 
-def own_experts(x, og, g, w_gate, w_up, w_down):
+def own_experts(x, back, g, w_gate, w_up):
     rows, width = x.shape
     experts, _, hidden = w_gate.shape
     up_spec = pl.BlockSpec((2, width, hidden), lambda p: (p, 0, 0))
@@ -121,48 +181,48 @@
         grid=(experts // 2,),
         in_specs=[
             whole(x),
-            whole(og),
+            pl.BlockSpec((None, rows, 2 * hidden), lambda p: (p, 0, 0)),
             whole(g),
             up_spec,
             up_spec,
-            pl.BlockSpec((2, hidden, width), lambda p: (p, 0, 0)),
         ],
         out_specs=[
-            pl.BlockSpec((rows, 2 * hidden), lambda p: (0, p)),
-            pl.BlockSpec((rows, 4 * hidden), lambda p: (0, p)),
-            pl.BlockSpec((rows, width), lambda p: (0, 0)),
+            pl.BlockSpec((None, rows, 2 * hidden), lambda p: (p, 0, 0)),
+            pl.BlockSpec((None, rows, 4 * hidden), lambda p: (p, 0, 0)),
+            pl.BlockSpec((rows // 2, width), lambda p: (0, 0)),
+            pl.BlockSpec((rows // 2, width), lambda p: (0, 0)),
         ],
         out_shape=[
-            jax.ShapeDtypeStruct((rows, experts * hidden), bfloat),
-            jax.ShapeDtypeStruct((rows, 2 * experts * hidden), bfloat),
-            jax.ShapeDtypeStruct((rows, width), wide),
+            jax.ShapeDtypeStruct((experts // 2, rows, 2 * hidden), bfloat),
+            jax.ShapeDtypeStruct((experts // 2, rows, 4 * hidden), bfloat),
+            jax.ShapeDtypeStruct((rows // 2, width), wide),
+            jax.ShapeDtypeStruct((rows // 2, width), wide),
         ],
         compiler_params=pltpu.CompilerParams(
             dimension_semantics=("arbitrary",), vmem_limit_bytes=40 * 2**20
         ),
         cost_estimate=BRIEF,
         name="own_experts",
-    )(x, og, g, w_gate, w_up, w_down)
+    )(x, back, g, w_gate, w_up)
 
 
 def grads_body(first, parts_n, *refs):
-    x_refs, og_refs, g_refs, xt_refs, ogt_refs = (
+    x_refs, g_refs, xt_refs, ogt_refs, back_refs = (
         refs[parts_n * i : parts_n * (i + 1)] for i in range(5)
     )
-    own_xt, own_ogt, own_ga, own_gu, wg_ref, wu_ref, wd_ref, keep, send = refs[
-        5 * parts_n : 5 * parts_n + 9
+    own_xt, own_ogt, own_ga, own_gu, wg_ref, wu_ref, keep, send = refs[
+        5 * parts_n : 5 * parts_n + 8
     ]
     s_refs, sa_ref = refs[-3:-1], refs[-1]
     pair = pl.program_id(0)
     hidden = wg_ref.shape[2]
     w_pair = [jnp.concatenate([wg_ref[j], wu_ref[j]], axis=1) for j in range(2)]
-    wd2 = wd_ref[...].reshape(2 * hidden, wd_ref.shape[2])
     rows = x_refs[0].shape[0]
 
     for n in range(parts_n):
         to = slice(n * rows, (n + 1) * rows)
         cols = gate_columns(g_refs[n][...], 2 * (pair + first))
-        parts = expert_parts(x_refs[n][...], og_refs[n][...], cols, w_pair, wd2)
+        parts = expert_parts(x_refs[n][...], back_refs[n][...], cols, w_pair)
         for j in range(2):
             ga, gg, ug = parts[j]
             sa_ref[to, j * hidden : (j + 1) * hidden] = ga
@@ -180,43 +240,47 @@
         lanes = slice(2 * j * hidden, 2 * (j + 1) * hidden)
         grad = total(xt_refs, own_xt, s_refs[j], own_gu[:, lanes])
         for i in range(2):
-            keep[j, i] = grad[:shard, i * hidden : (i + 1) * hidden]
-            send[j, i] = grad[shard:, i * hidden : (i + 1) * hidden]
+            keep[i, j] = grad[:shard, i * hidden : (i + 1) * hidden]
+            send[i, j] = grad[shard:, i * hidden : (i + 1) * hidden]
     down = total(ogt_refs, own_ogt, sa_ref, own_ga[...])
     for j in range(2):
         turned = down[:, j * hidden : (j + 1) * hidden].T
-        keep[j, 2] = turned[:, :shard]
-        send[j, 2] = turned[:, shard:]
-
-
-def expert_grads(first_expert, count, x, og, g, xt, ogt, own_xt, own_ogt, own_ga, own_gu, weights):
+        keep[2, j] = turned[:, :shard]
+        send[2, j] = turned[:, shard:]
+
+
+def expert_grads(first_expert, count, x, g, xt, ogt, back, own_xt, own_ogt, own_ga, own_gu, weights):
     rows, width = x[0].shape
-    w_gate, w_up, w_down = weights
+    w_gate, w_up = weights
     _, _, hidden = w_gate.shape
-    own_rows = own_ga.shape[0]
+    own_rows = own_ga.shape[1]
     all_rows = len(x) * rows
     shard = own_xt.shape[0] // 2
     first = first_expert // 2
     up_spec = pl.BlockSpec((2, width, hidden), lambda p: (p + first, 0, 0))
-    out_spec = pl.BlockSpec((2, 3, shard, hidden), lambda p: (p, 0, 0, 0))
-    out_shape = jax.ShapeDtypeStruct((count, 3, shard, hidden), wide)
-    resident = (*x, *og, *g, *xt, *ogt, own_xt, own_ogt)
+    out_spec = pl.BlockSpec((3, 2, shard, hidden), lambda p: (0, p, 0, 0))
+    out_shape = jax.ShapeDtypeStruct((3, count, shard, hidden), wide)
+    resident = (*x, *g, *xt, *ogt)
+    pair_spec = lambda n: pl.BlockSpec((None, n, 2 * hidden), lambda p: (p + first, 0, 0))
     return pl.pallas_call(
         functools.partial(grads_body, first, len(x)),
         grid=(count // 2,),
         in_specs=[whole(a) for a in resident]
-        + [pl.BlockSpec((own_rows, 2 * hidden), lambda p: (0, p + first))]
-        + [pl.BlockSpec((own_rows, 4 * hidden), lambda p: (0, p + first))]
-        + [up_spec, up_spec, pl.BlockSpec((2, hidden, width), lambda p: (p + first, 0, 0))],
+        + [pair_spec(rows)] * len(back)
+        + [whole(own_xt), whole(own_ogt), pair_spec(own_rows)]
+        + [pl.BlockSpec((None, own_rows, 4 * hidden), lambda p: (p + first, 0, 0))]
+        + [up_spec, up_spec],
         out_specs=[out_spec] * 2,
         out_shape=[out_shape] * 2,
         scratch_shapes=[pltpu.VMEM((all_rows, 2 * hidden), bfloat)] * 3,
         compiler_params=pltpu.CompilerParams(
-            dimension_semantics=("arbitrary",), vmem_limit_bytes=56 * 2**20
+            dimension_semantics=("arbitrary",), vmem_limit_bytes=48 * 2**20
         ),
-        cost_estimate=BRIEF,
+        cost_estimate=pl.CostEstimate(
+            flops=count * 2**32, bytes_accessed=count * 2**22, transcendentals=0
+        ),
         name="expert_grads",
-    )(*resident, own_ga, own_gu, *weights)
+    )(*resident, *back, own_xt, own_ogt, own_ga, own_gu, *weights)
 
 
 def prepare_body(normed, place_ref, mine_ref, other_ref, gain_ref, x_ref, t_ref):
@@ -380,20 +444,18 @@
             x_side == 0, jnp.concatenate([mine, other], 0), jnp.concatenate([other, mine], 0)
         )
 
-    def sum_z(blocks):
+    def send_z(split):
         z = dp_place // 2
+        place = lambda k: lax.dynamic_index_in_dim(split, (z + k) % 4, 0, False)
+        return [place(0)] + [along_z(place(k), k) for k in (1, 2, 3)]
+
+    def split_y(blocks):
         split = blocks.reshape((4, 2) + blocks.shape[1:])
-        total = lax.dynamic_index_in_dim(split, z, 0, False)
-        for k in (1, 2, 3):
-            total = total + along_z(lax.dynamic_index_in_dim(split, (z + k) % 4, 0, False), k)
-        return total
-
-    def sum_y(blocks):
         y = dp_place % 2
-        kept = lax.dynamic_index_in_dim(blocks, y, 0, False)
-        return kept + lax.ppermute(
-            lax.dynamic_index_in_dim(blocks, 1 - y, 0, False), "dp", y_pairs
-        )
+        return [lax.dynamic_index_in_dim(split, place, 1, False) for place in (y, 1 - y)]
+
+    def send_y(v):
+        return lax.ppermute(v, "dp", y_pairs)
 
     out_wide = out_grad.astype(wide)
     lane = jnp.arange(EXPERTS, dtype=jnp.int32)
@@ -473,32 +535,33 @@
     )
     own_og, own_ogt = ready(og_mine, og_other, normed=False)
     own_gates = jnp.concatenate([gates_mine, gates_other], 0)
+    own_back = back_through_down(own_og, w_down)
     if small:
         mixed_low, og_z[1] = together(mixed_low, og_z[1])
     attn_both = dot_nn(my_half(mixed_low), w_out) + swap_core(
         dot_nn(other_half(mixed_low), w_out)
     )
-    attention = after(attn_both + swap_x(attn_both), own_og, own_ogt, own_gates)
+    attention, own_back, own_ogt, own_gates = together(
+        attn_both + swap_x(attn_both), own_back, own_ogt, own_gates
+    )
     if small:
         attention, og_z[2] = together(attention, og_z[2])
     hidden = my_half(tokens_wide) + attention
     hidden_other = swap_core(hidden)
-    weights = (w_gate, w_up, w_down)
+    weights = (w_gate, w_up)
     own_x, own_xt = ready(hidden, hidden_other, normed=True)
-    ga, gu, n_part = own_experts(own_x, own_og, own_gates, *weights)
+    ga, gu, n_part, n_other = own_experts(own_x, own_back, own_gates, *weights)
     if small:
         z_hidden = {2: along_z(my_quarter(hidden), 2)}
         og_x = {k: swap_x(og_z[k]) for k in (1, 2)}
-        n_part, z_hidden[2], og_z[3], og_x[1], og_x[2] = together(
-            n_part, z_hidden[2], og_z[3], og_x[1], og_x[2]
-        )
-
-    n_both = n_part[:half] + swap_core(n_part[half:])
-    normed2_grad = n_both + swap_x(n_both)
-    w_down2 = w_down.reshape(-1, width)
-    e_both = dot_nn(ga[:half], w_down2) + swap_core(dot_nn(ga[half:], w_down2))
-    waiting = [e_both]
+        n_part, n_other, z_hidden[2], og_x[1], og_x[2] = together(
+            n_part, n_other, z_hidden[2], og_x[1], og_x[2]
+        )
+
+    n_both = n_part + swap_core(n_other)
+    e_mine, e_other = down_products(ga, w_down)
     if small:
+
         def og_part(k):
             og_h = join_x(og_z[k][:quarter], og_x[k][:quarter])
             gates_h = join_x(og_z[k][quarter:], og_x[k][quarter:])
@@ -506,24 +569,36 @@
             arrived = swap_core(og_h)
             prepared = ready(og_h, arrived, normed=False)
             both_gates = jnp.concatenate([gates_h, arrived[half:]], 0).reshape(-1, EXPERTS)
-            return (*prepared, both_gates)
-
-        og_parts = {k: og_part(k) for k in (1, 2)}
-        z_hidden[1] = along_z(after(hidden, n_part), 1)
-        waiting += [z_hidden[1], *og_parts[1], *og_parts[2]]
-    normed2_grad, e_both, *waited = together(normed2_grad, *waiting)
-    if small:
-        z_hidden[1] = waited[0]
-        og_parts = {1: waited[1:4], 2: waited[4:7]}
+            return [back_through_down(prepared[0], w_down), prepared[1], both_gates]
+
+        n_first = swap_x(n_both[:quarter])
+        e_mine, e_other, n_first, og_z[3], og_x[1], og_x[2] = together(
+            e_mine, e_other, n_first, og_z[3], og_x[1], og_x[2]
+        )
+        n_second = swap_x(after(n_both[quarter:], n_first))
+        z_first = {1: along_z(after(hidden[:quarter], og_z[3]), 1)}
+        og_parts = {2: og_part(2)}
+        og_parts[2][0], n_second, og_x[1], z_first[1] = together(
+            og_parts[2][0], n_second, og_x[1], z_first[1]
+        )
+        z_second = {1: along_z(after(hidden[quarter:], z_first[1]), 1)}
+        n_arrived = jnp.concatenate([n_first, n_second], 0)
+    else:
+        n_arrived = swap_x(n_both)
+    normed2_grad = n_both + n_arrived
     hidden_part, gain2_grad = norm_backward(hidden, norm2_gain, normed2_grad)
     hidden_grad = my_half(out_wide) + hidden_part
-    attn_grad = natural(hidden_grad.astype(bfloat), rounded(swap_core(hidden_grad)))
+    other_grad = swap_core(hidden_grad)
+    attn_grad = natural(hidden_grad.astype(bfloat), rounded(other_grad))
     if small:
-        z_hidden[3] = along_z(after(hidden, normed2_grad), 3)
-        og_x[3] = swap_x(after(og_z[3], normed2_grad))
-        hidden_x = swap_x(after(z_hidden[2], normed2_grad))
-
-    grad_w_out = jnp.einsum("tc,td->cd", mixed_low, attn_grad, preferred_element_type=wide)
+        og_x[3] = swap_x(after(og_z[3], n_second))
+        hidden_x = swap_x(after(z_hidden[2], n_second))
+        og_parts[1] = og_part(1)
+        attn_grad, og_parts[1][0], z_second[1] = together(
+            attn_grad, og_parts[1][0], z_second[1]
+        )
+        z_first[3] = along_z(after(hidden[:quarter], z_second[1]), 3)
+
     mixed_grad = dot_nt(attn_grad, w_out).astype(bfloat)
     mixed_grad = mixed_grad.reshape(row_count, local_groups, per_group, HEAD_DIM)
     key_grad = jnp.zeros((row_count, local_groups, HEAD_DIM), wide)
@@ -562,59 +637,87 @@
     )
     w_qkv = jnp.concatenate([w_query, w_key, w_value], 1)
     if small:
-        qkv_low, og_x[3], hidden_x, z_hidden[3] = together(
-            qkv_low, og_x[3], hidden_x, z_hidden[3]
-        )
+        qkv_low, og_x[3], hidden_x, z_first[3] = together(
+            qkv_low, og_x[3], hidden_x, z_first[3]
+        )
+        z_second[3] = along_z(after(hidden[quarter:], z_first[3]), 3)
     t_both = dot_nt(my_half(qkv_low), w_qkv) + swap_core(dot_nt(other_half(qkv_low), w_qkv))
-    normed1_grad = t_both + swap_x(t_both)
-    tokens_mine = my_half(tokens_wide)
-    tokens_part, gain1_grad = norm_backward(tokens_mine, norm1_gain, normed1_grad)
-    tokens_half = hidden_grad + tokens_part
-    expert_total = e_both + swap_x(after(e_both, t_both))
-    block_mine = hidden + expert_total
-
-    grad_w_qkv = jnp.einsum("td,tc->dc", normed1_low, qkv_low, preferred_element_type=wide)
-    gain2_grad = gain2_grad + swap_core(gain2_grad)
-    joined = jnp.concatenate(
-        [
-            grad_w_qkv.reshape(dp_size, grad_w_qkv.shape[1], shard),
-            grad_w_out.reshape(w_out.shape[0], dp_size, shard).transpose(1, 0, 2),
-            jnp.broadcast_to(gain2_grad.reshape(dp_size, 1, shard), (dp_size, 8, shard)),
-        ],
-        1,
-    )
-    gain1_grad = (gain1_grad + swap_core(gain1_grad)).reshape(dp_size, -1)
+    t_arrived = swap_x(t_both)
+
+    def send_expert_part(*start):
+        e_both = after(e_mine, *start) + swap_core(after(e_other, *start))
+        return e_both, [swap_x(e_both[:quarter]), swap_x(e_both[quarter:])]
+
+
+    def finish_tokens(t_arrived):
+        tokens_part, gain1_grad = norm_backward(
+            my_half(tokens_wide), norm1_gain, t_both + t_arrived
+        )
+        gain1_grad = (gain1_grad + swap_core(gain1_grad)).reshape(dp_size, -1)
+        return hidden_grad + tokens_part, gain1_grad
+
+    def join_grads(normed1_low, qkv_low, mixed_low, attn_grad, gain2_grad):
+        grad_w_out = jnp.einsum("tc,td->cd", mixed_low, attn_grad, preferred_element_type=wide)
+        grad_w_qkv = jnp.einsum("td,tc->dc", normed1_low, qkv_low, preferred_element_type=wide)
+        gain2_grad = gain2_grad + swap_core(gain2_grad)
+        return jnp.concatenate(
+            [
+                grad_w_qkv.reshape(dp_size, grad_w_qkv.shape[1], shard),
+                grad_w_out.reshape(w_out.shape[0], dp_size, shard).transpose(1, 0, 2),
+                jnp.broadcast_to(gain2_grad.reshape(dp_size, 1, shard), (dp_size, 8, shard)),
+            ],
+            1,
+        )
 
     if small:
         og_parts[3] = og_part(3)
         hidden_parts = {}
         for k in (1, 2, 3):
-            hidden_h = z_hidden[k] if k != 2 else join_x(z_hidden[2], hidden_x)
-            hidden_parts[k] = ready(hidden_h, swap_core(hidden_h), normed=True)
+            if k == 2:
+                hidden_h = join_x(z_hidden[2], hidden_x)
+            else:
+                hidden_h = jnp.concatenate([z_first[k], z_second[k]], 0)
+            hidden_parts[k] = list(ready(hidden_h, swap_core(hidden_h), normed=True))
+            if k == 2:
+                hidden_parts[2][0], z_second[3] = together(hidden_parts[2][0], z_second[3])
         shifts = (1, 2, 3)
         xs = [hidden_parts[k][0] for k in shifts]
         xs = list(lax.optimization_barrier((*xs, t_both))[:3])
         pieces = []
         first = 0
-        joined = sum_z(joined)
         for number, count in enumerate(CHUNK_SIZES):
+            if number == 0:
+                joined = split_y(join_grads(normed1_low, qkv_low, mixed_low, attn_grad, gain2_grad))
+                *xs, joined[0], joined[1] = together(*xs, *joined)
+                joined[1] = send_y(joined[1])
             if number == 1:
-                *xs, tokens_half, joined = together(*xs, tokens_half, joined)
-                joined = sum_y(joined)
-                gain1 = sum_z(gain1_grad)
+                keep, send, joined[1] = together(keep, send, joined[1])
+                pieces[0][:2] = keep, send
+                joined = send_z(joined[0] + joined[1])
             if number == 2:
-                *xs, block_mine, gain1, pieces[0] = together(*xs, block_mine, gain1, pieces[0])
-                gain1 = sum_y(gain1)
+                keep, send, t_arrived, *joined, pieces[0][2] = together(
+                    keep, send, t_arrived, *joined, pieces[0][2]
+                )
+                pieces[1][:2] = keep, send
+                joined = sum(joined)
+                e_both, e_arrived = send_expert_part(keep)
+                tokens_half, gain1_grad = finish_tokens(t_arrived)
+                *xs, tokens_half, gain1_grad = together(*xs, tokens_half, gain1_grad)
+                gain1 = send_z(gain1_grad.reshape(4, 2, -1))
             if number == 3:
-                *xs, joined, gain1, pieces[1] = together(*xs, joined, gain1, pieces[1])
+                keep, send, e_arrived[0], pieces[1][2], *gain1 = together(
+                    keep, send, e_arrived[0], pieces[1][2], *gain1
+                )
+                pieces[2][:2] = keep, send
+                gain1 = sum(gain1)
             keep, send = expert_grads(
                 first,
                 count,
                 xs,
-                [og_parts[k][0] for k in shifts],
                 [og_parts[k][2] for k in shifts],
                 [hidden_parts[k][1] for k in shifts],
                 [og_parts[k][1] for k in shifts],
+                [og_parts[k][0] for k in shifts],
                 own_xt,
                 own_ogt,
                 ga,
@@ -622,20 +725,32 @@
                 weights,
             )
             first += count
-            pieces.append(keep + lax.ppermute(send, "dp", y_pairs))
+            pieces.append([keep, send, send_y(send)])
+        keep, e_arrived[1], pieces[2][2] = together(keep, e_arrived[1], pieces[2][2])
+        pieces[-1][0] = keep
+        block_mine = hidden + (e_both + jnp.concatenate(e_arrived, 0))
+        mine_y, other_y = (
+            lax.dynamic_index_in_dim(gain1, place, 0, False)
+            for place in (dp_place % 2, 1 - dp_place % 2)
+        )
+        gain1 = mine_y + send_y(other_y)
         block_out = place_halves(block_mine, swap_core(block_mine), core)
         tokens_grad = place_halves(tokens_half, swap_core(tokens_half), core)
-        *pieces, block_out, tokens_grad = together(*pieces, block_out, tokens_grad)
+        pieces[-1][2], block_out, tokens_grad = together(pieces[-1][2], block_out, tokens_grad)
         grad_w_gate, grad_w_up, grad_w_down = (
-            jnp.concatenate([c[:, i] for c in pieces], 0) for i in range(3)
+            jnp.concatenate([c[0][i] + c[2][i] for c in pieces], 0) for i in range(3)
         )
     else:
+        joined = join_grads(normed1_low, qkv_low, mixed_low, attn_grad, gain2_grad)
         joined = lax.psum_scatter(joined, "dp", scatter_dimension=0, tiled=True)[0]
+        tokens_half, gain1_grad = finish_tokens(t_arrived)
         gain1 = lax.psum_scatter(gain1_grad, "dp", scatter_dimension=0, tiled=True)[0]
+        e_both, e_arrived = send_expert_part(t_both)
+        block_mine = hidden + (e_both + jnp.concatenate(e_arrived, 0))
         block_out = place_halves(block_mine, swap_core(block_mine), core)
         tokens_grad = place_halves(tokens_half, swap_core(tokens_half), core)
-        ga = ga.reshape(row_count, EXPERTS, -1)
-        gu = gu.reshape(row_count, EXPERTS, 2, -1)
+        ga = ga.transpose(1, 0, 2).reshape(row_count, EXPERTS, -1)
+        gu = gu.transpose(1, 0, 2).reshape(row_count, EXPERTS, 2, -1)
         grad_w_gate = jnp.einsum("td,tef->edf", own_x, gu[:, :, 0], preferred_element_type=wide)
         grad_w_up = jnp.einsum("td,tef->edf", own_x, gu[:, :, 1], preferred_element_type=wide)
         grad_w_down = jnp.einsum("tef,td->efd", ga, own_og, preferred_element_type=wide)
@@ -643,7 +758,7 @@
         grad_w_up = lax.psum_scatter(grad_w_up, "dp", scatter_dimension=1, tiled=True)
         grad_w_down = lax.psum_scatter(grad_w_down, "dp", scatter_dimension=2, tiled=True)
 
-    qkv_rows = grad_w_qkv.shape[1]
+    qkv_rows = qkv_low.shape[1]
     grad_w_qkv = joined[:qkv_rows].reshape(shard, -1)
     grad_w_out = joined[qkv_rows : qkv_rows + w_out.shape[0]]
     gain2 = joined[-8]

time: 635 us -> 616 us (0.970)
  matrix products: 58.7 us -> 40.2 us
  Pallas kernels: 275 us -> 288 us
  local copies, waits for them, and re-layouts: 70.1 us -> 62 us
  other arithmetic: 75.4 us -> 67.7 us
    pallas_call x1 -> x6, Pallas kernels: 66.4 us -> 120 us  [the longest x4 57.8 us: back_through_down(): pl.pallas_call(back_body, grid=(experts // 4,), in_specs=[whole(og), pl.B...]
    pallas_call x4, Pallas kernels: 158 us -> 117 us  [expert_grads(): pl.pallas_call(functools.partial(grads_body, first, len(x)), grid=(count...]
    ppermute x8 -> x10, waiting for transfers between devices: 74.8 us -> 35.5 us  [swap_x(): return lax.ppermute(v, 'tensor', X_PAIRS)]
    ppermute x12 -> x14, waiting for transfers between devices: 2.48 us -> 25.6 us  [along_z(): return lax.ppermute(v, 'dp', z_shifts[k])]
    dot_general x7 -> x5, matrix products: 22.4 us -> 5.69 us  [dot_nn(): return jnp.dot(a, b, preferred_element_type=wide)]
    add x15 -> x14, other arithmetic: 29 us -> 20.8 us  [the longest x4 9.36 us: per_device(): c[0][i] + c[2][i]]
    pallas_call x3 -> x0, local copies, waits for them, and re-layouts: 7.18 us -> none  [expert_grads(): pl.pallas_call(functools.partial(grads_body, first, len(x)), grid=(count...]
    ppermute x12 -> x14, starting transfers between devices: 22.2 us -> 26.2 us  [along_z(): return lax.ppermute(v, 'dp', z_shifts[k])]
  transfers between devices with their start and end apart: 42 -> 46, of which waited for: 9 -> 18; matrix products, arithmetic and copies ran while one was open for 25% -> 21% of each run, Pallas kernels for 44% -> 48%
where the time goes in v3:
time: 616 us; the launch traced here: 604 us
  Pallas kernels  288 us (47%)
  waiting for transfers between devices  96.3 us (16%)
  other arithmetic  67.7 us (11%)
  local copies, waits for them, and re-layouts  62 us (10%)
  starting transfers between devices  46.6 us (8%)
  matrix products  40.2 us (7%)
    pallas_call x4, Pallas kernels, expert_grads(): pl.pallas_call(functools.partial(grads_body, first, len(x)), grid=(count...  117 us
    pallas_call x4, Pallas kernels, back_through_down(): pl.pallas_call(back_body, grid=(experts // 4,), in_specs=[whole(og), pl.B...  57.8 us
    pallas_call x1, Pallas kernels, own_experts(): pl.pallas_call(own_body, grid=(experts // 2,), in_specs=[whole(x), pl.Blo...  47.7 us
    pallas_call x8, Pallas kernels, prepare(): pl.pallas_call(functools.partial(prepare_body, normed), grid_spec=pltpu.P...  40.3 us
    ppermute x10, waiting for transfers between devices, swap_x(): return lax.ppermute(v, 'tensor', X_PAIRS)  35.5 us
    ppermute x14, starting transfers between devices, along_z(): return lax.ppermute(v, 'dp', z_shifts[k])  26.2 us
    ppermute x14, waiting for transfers between devices, along_z(): return lax.ppermute(v, 'dp', z_shifts[k])  25.6 us
    ppermute x6, waiting for transfers between devices, send_y(): return lax.ppermute(v, 'dp', y_pairs)  24.9 us
  transfers between devices with their start and end apart: 46, of which 18 were waited for; matrix products, arithmetic and copies ran while one was open for 21% of the time, Pallas kernels for 48%

profile of v3, /device:TPU:0, one launch (start us, length us, event | category | flops | bytes accessed | tf_op | source)
XLA Modules:
  0.0 603.7 jit_solution(2916557117165806166)
XLA Ops:
  57.2 14.4 %back_through_down.4.back_ref = bf16[16,1024,256]{2,1,0:T(8,128)(2,1)} custom-call(bf16[1024,1024]{1,0:T(8,128)(2,1)} %get-tuple-element.118.og_ref, bf16[32,128,1024]{2,1,0:T(8,128)(2,1)} %wd_ref.9), custom_call_target="tpu_custom_call" | custom-call | flops 1048576 | bytes 1048576 | tf_op jit(solution)/shard_map/back_through_down/pallas_call | solution.py:122
  71.7 18.7 %collective-permute-done.2 = f32[512,1024]{1,0:T(8,128)} collective-permute-done((f32[512,1024]{1,0:T(8,128)}, f32[512,1024]{1,0:T(8,128)}, u32[]{:S(2)}, u32[]{:S(2)}) %collective-permute-start.2) | collective-permute-done | bytes 2097184 | tf_op jit(solution)/shard_map/ppermute | solution.py:422
  99.2 5.1 prepare.9
  105.8 47.7 %own_experts.1 = (bf16[16,1024,256]{2,1,0:T(8,128)(2,1)}, bf16[16,1024,512]{2,1,0:T(8,128)(2,1)}, f32[512,1024]{1,0:T(8,128)S(1)}, f32[512,1024]{1,0:T(8,128)S(1)}) custom-call(bf16[1024,1024]{1,0:T(8,128)(2,1)S(1)} %copy-done.2, bf16[16,1024,256]{2,1,0:T(8,128)(2,1)} %back_through_down.4.back_ref, f32[1024,32]{1,0:T(8,128)S(1)} %copy.63.g_ref, ...), custom_call_target="tpu_custom_call" | custom-call | flops 1048576 | bytes 1048576 | tf_op jit(solution)/shard_map/own_experts/pallas_call | solution.py:179
  163.2 14.5 %down_products.1 = (f32[512,1024]{1,0:T(8,128)}, f32[512,1024]{1,0:T(8,128)}) custom-call(bf16[16,1024,256]{2,1,0:T(8,128)(2,1)} %get-tuple-element.126.ga_ref.refs_17_, bf16[32,128,1024]{2,1,0:T(8,128)(2,1)} %wd_ref.9), custom_call_target="tpu_custom_call" | custom-call | flops 1048576 | bytes 1048576 | tf_op jit(solution)/shard_map/down_products/pallas_call | solution.py:154
  198.4 14.5 %back_through_down.5.refs_13_ = bf16[16,1024,256]{2,1,0:T(8,128)(2,1)} custom-call(bf16[1024,1024]{1,0:T(8,128)(2,1)} %get-tuple-element.137.og_ref, bf16[32,128,1024]{2,1,0:T(8,128)(2,1)} %wd_ref.9), custom_call_target="tpu_custom_call" | custom-call | flops 1048576 | bytes 1048576 | tf_op jit(solution)/shard_map/back_through_down/pallas_call | solution.py:122
  240.5 14.5 %back_through_down.6.refs_12_ = bf16[16,1024,256]{2,1,0:T(8,128)(2,1)} custom-call(bf16[1024,1024]{1,0:T(8,128)(2,1)} %get-tuple-element.146.og_ref, bf16[32,128,1024]{2,1,0:T(8,128)(2,1)} %wd_ref.9), custom_call_target="tpu_custom_call" | custom-call | flops 1048576 | bytes 1048576 | tf_op jit(solution)/shard_map/back_through_down/pallas_call | solution.py:122
  256.5 5.3 fusion.3
  281.7 11.0 %collective-permute-done.20 = f32[256,1024]{1,0:T(8,128)} collective-permute-done((f32[256,1024]{1,0:T(8,128)}, f32[256,1024]{1,0:T(8,128)}, u32[]{:S(2)}, u32[]{:S(2)}) %collective-permute-start.20) | collective-permute-done | bytes 1048608 | tf_op jit(solution)/shard_map/ppermute | solution.py:440
  315.5 5.1 prepare.13
  320.6 5.3 collective-permute-done.22
  347.5 5.2 prepare.12
  359.3 5.0 prepare.15
  364.3 14.4 %back_through_down.7.refs_14_ = bf16[16,1024,256]{2,1,0:T(8,128)(2,1)} custom-call(bf16[1024,1024]{1,0:T(8,128)(2,1)} %get-tuple-element.178.og_ref, bf16[32,128,1024]{2,1,0:T(8,128)(2,1)} %wd_ref.9), custom_call_target="tpu_custom_call" | custom-call | flops 1048576 | bytes 1048576 | tf_op jit(solution)/shard_map/back_through_down/pallas_call | solution.py:122
  378.7 5.2 prepare.14
  390.6 29.4 %expert_grads.5 = (f32[3,8,128,128]{3,2,1,0:T(8,128)}, f32[3,8,128,128]{3,2,1,0:T(8,128)}) custom-call(bf16[1024,1024]{1,0:T(8,128)(2,1)} %get-tuple-element.190.refs_0_, bf16[1024,1024]{1,0:T(8,128)(2,1)} %get-tuple-element.191.refs_1_, bf16[1024,1024]{1,0:T(8,128)(2,1)} %get-tuple-element.192.refs_2_, f32[1024,32]{1,0:T(8,128)S(1)} %reshape.333.refs_3_, ...), custom_call_target="tpu_custom_call" | custom-call | flops 34359738368 | bytes 33554432 | tf_op jit(solution)/shard_map/expert_grads/pallas_call | solution.py:265
  426.8 35.3 %expert_grads.4 = (f32[3,10,128,128]{3,2,1,0:T(8,128)}, f32[3,10,128,128]{3,2,1,0:T(8,128)}) custom-call(bf16[1024,1024]{1,0:T(8,128)(2,1)} %get-tuple-element.190.refs_0_, bf16[1024,1024]{1,0:T(8,128)(2,1)} %get-tuple-element.191.refs_1_, bf16[1024,1024]{1,0:T(8,128)(2,1)} %get-tuple-element.192.refs_2_, f32[1024,32]{1,0:T(8,128)S(1)} %reshape.333.refs_3_, ...), custom_call_target="tpu_custom_call" | custom-call | flops 42949672960 | bytes 41943040 | tf_op jit(solution)/shard_map/expert_grads/pallas_call | solution.py:265
  477.1 29.4 %expert_grads.7 = (f32[3,8,128,128]{3,2,1,0:T(8,128)}, f32[3,8,128,128]{3,2,1,0:T(8,128)}) custom-call(bf16[1024,1024]{1,0:T(8,128)(2,1)} %get-tuple-element.190.refs_0_, bf16[1024,1024]{1,0:T(8,128)(2,1)} %get-tuple-element.191.refs_1_, bf16[1024,1024]{1,0:T(8,128)(2,1)} %get-tuple-element.192.refs_2_, f32[1024,32]{1,0:T(8,128)S(1)} %reshape.333.refs_3_, ...), custom_call_target="tpu_custom_call" | custom-call | flops 34359738368 | bytes 33554432 | tf_op jit(solution)/shard_map/expert_grads/pallas_call | solution.py:265
  510.2 23.4 %expert_grads.6 = (f32[3,6,128,128]{3,2,1,0:T(8,128)}, f32[3,6,128,128]{3,2,1,0:T(8,128)}) custom-call(bf16[1024,1024]{1,0:T(8,128)(2,1)} %get-tuple-element.190.refs_0_, bf16[1024,1024]{1,0:T(8,128)(2,1)} %get-tuple-element.191.refs_1_, bf16[1024,1024]{1,0:T(8,128)(2,1)} %get-tuple-element.192.refs_2_, f32[1024,32]{1,0:T(8,128)S(1)} %reshape.333.refs_3_, ...), custom_call_target="tpu_custom_call" | custom-call | flops 25769803776 | bytes 25165824 | tf_op jit(solution)/shard_map/expert_grads/pallas_call | solution.py:265
  534.2 10.3 %collective-permute-done.42 = f32[3,8,128,128]{3,2,1,0:T(8,128)S(1)} collective-permute-done((f32[3,8,128,128]{3,2,1,0:T(8,128)}, f32[3,8,128,128]{3,2,1,0:T(8,128)S(1)}, u32[]{:S(2)}, u32[]{:S(2)}) %collective-permute-start.42) | collective-permute-done | bytes 1572896 | tf_op jit(solution)/shard_map/ppermute | solution.py:458
  544.5 11.5 %collective-permute-done.41 = f32[256,1024]{1,0:T(8,128)} collective-permute-done((f32[256,1024]{1,0:T(8,128)S(1)}, f32[256,1024]{1,0:T(8,128)}, u32[]{:S(2)}, u32[]{:S(2)}) %collective-permute-start.41) | collective-permute-done | bytes 1048608 | tf_op jit(solution)/shard_map/ppermute | solution.py:422
  565.9 5.2 place_halves.3
  576.7 14.3 %collective-permute-done.45 = f32[128]{0:T(128)S(1)} collective-permute-done((f32[128]{0:T(128)S(1)}, f32[128]{0:T(128)S(1)}, u32[]{:S(2)}, u32[]{:S(2)}) %collective-permute-start.45) | collective-permute-done | bytes 544 | tf_op jit(solution)/shard_map/ppermute | solution.py:458
  591.5 5.3 place_halves.2
  (418 shorter events, 251.3 us)
Async XLA Ops:
  42.3 48.0 %collective-permute-start.2 = (f32[512,1024]{1,0:T(8,128)}, f32[512,1024]{1,0:T(8,128)}, u32[]{:S(2)}, u32[]{:S(2)}) collective-permute-start(f32[512,1024]{1,0:T(8,128)} %convolution_add_fusion.1), channel_id=1, source_target_pairs={{0,2},{1,3},{2,0},{3,1},{4,6},{5,7},{6,4},{7,5},{8,10},{9,11},{10,... | collective-permute-start | bytes 6291464 | tf_op jit(solution)/shard_map/ppermute | solution.py:422
  43.8 49.6 %collective-permute-start.3 = (f32[264,1024]{1,0:T(8,128)}, f32[264,1024]{1,0:T(8,128)}, u32[]{:S(2)}, u32[]{:S(2)}) collective-permute-start(f32[264,1024]{1,0:T(8,128)} %pad_maximum_fusion.7), channel_id=1, source_target_pairs={{0,16},{4,20},{8,24},{12,28},{16,0},{20,4},{24,8},{28,12},{1,17},{... | collective-permute-start | bytes 3244040 | tf_op jit(solution)/shard_map/ppermute | solution.py:440
  94.5 59.0 %collective-permute-start.6 = (f32[264,1024]{1,0:T(8,128)}, f32[264,1024]{1,0:T(8,128)}, u32[]{:S(2)}, u32[]{:S(2)}) collective-permute-start(f32[264,1024]{1,0:T(8,128)} %collective-permute-done), channel_id=1, source_target_pairs={{0,2},{1,3},{2,0},{3,1},{4,6},{5,7},{6,4},{7,5},{8,10},{9,11},{10,... | collective-permute-start | bytes 3244040 | tf_op jit(solution)/shard_map/ppermute | solution.py:422
  95.5 58.0 %collective-permute-start.7 = (f32[264,1024]{1,0:T(8,128)}, f32[264,1024]{1,0:T(8,128)}, u32[]{:S(2)}, u32[]{:S(2)}) collective-permute-start(f32[264,1024]{1,0:T(8,128)} %collective-permute-done.3), channel_id=1, source_target_pairs={{0,2},{1,3},{2,0},{3,1},{4,6},{5,7},{6,4},{7,5},{8,10},{9,11},{10,... | collective-permute-start | bytes 3244040 | tf_op jit(solution)/shard_map/ppermute | solution.py:422
  98.3 55.2 %collective-permute-start.5 = (f32[256,1024]{1,0:T(8,128)}, f32[256,1024]{1,0:T(8,128)}, u32[]{:S(2)}, u32[]{:S(2)}) collective-permute-start(f32[256,1024]{1,0:T(8,128)} %get-tuple-element.252), channel_id=1, source_target_pairs={{0,16},{4,20},{8,24},{12,28},{16,0},{20,4},{24,8},{28,12},{1,17},{... | collective-permute-start | bytes 3145736 | tf_op jit(solution)/shard_map/ppermute | solution.py:440
  229.2 52.5 %collective-permute-start.19 = (f32[256,1024]{1,0:T(8,128)}, f32[256,1024]{1,0:T(8,128)}, u32[]{:S(2)}, u32[]{:S(2)}) collective-permute-start(f32[256,1024]{1,0:T(8,128)} %collective-permute-done.5), channel_id=1, source_target_pairs={{0,2},{1,3},{2,0},{3,1},{4,6},{5,7},{6,4},{7,5},{8,10},{9,11},{10,... | collective-permute-start | bytes 3145736 | tf_op jit(solution)/shard_map/ppermute | solution.py:422
  230.2 51.5 %collective-permute-start.18 = (f32[264,1024]{1,0:T(8,128)}, f32[264,1024]{1,0:T(8,128)}, u32[]{:S(2)}, u32[]{:S(2)}) collective-permute-start(f32[264,1024]{1,0:T(8,128)} %collective-permute-done.10), channel_id=1, source_target_pairs={{0,2},{1,3},{2,0},{3,1},{4,6},{5,7},{6,4},{7,5},{8,10},{9,11},{10,... | collective-permute-start | bytes 3244040 | tf_op jit(solution)/shard_map/ppermute | solution.py:422
  307.2 40.3 %collective-permute-start.17 = (f32[512,1024]{1,0:T(8,128)}, f32[512,1024]{1,0:T(8,128)}, u32[]{:S(2)}, u32[]{:S(2)}) collective-permute-start(f32[512,1024]{1,0:T(8,128)} %constant_dynamic-update-slice_fusion.mine_ref), channel_id=1, source_target_pairs={{0,1},{1,0},{2,3},{3,2},{4,5},{5,4},{6,7},{7,6},{8,9},{9,8},{10,11... | collective-permute-start | bytes 6291464 | tf_op jit(solution)/shard_map/ppermute | solution.py:419
  311.6 41.1 %collective-permute-start.24 = (f32[512,1024]{1,0:T(8,128)}, f32[512,1024]{1,0:T(8,128)}, u32[]{:S(2)}, u32[]{:S(2)}) collective-permute-start(f32[512,1024]{1,0:T(8,128)} %fusion.46), channel_id=1, source_target_pairs={{0,1},{1,0},{2,3},{3,2},{4,5},{5,4},{6,7},{7,6},{8,9},{9,8},{10,11... | collective-permute-start | bytes 6291464 | tf_op jit(solution)/shard_map/ppermute | solution.py:419
  312.5 45.9 %collective-permute-start.26 = (f32[528,1024]{1,0:T(8,128)S(1)}, f32[528,1024]{1,0:T(8,128)}, u32[]{:S(2)}, u32[]{:S(2)}) collective-permute-start(f32[528,1024]{1,0:T(8,128)S(1)} %pad_maximum_fusion.3.mine_ref), channel_id=1, source_target_pairs={{0,1},{1,0},{2,3},{3,2},{4,5},{5,4},{6,7},{7,6},{8,9},{9,8},{10,11... | collective-permute-start | bytes 6488072 | tf_op jit(solution)/shard_map/ppermute | solution.py:419
  328.2 50.5 %collective-permute-start.23 = (f32[512,1024]{1,0:T(8,128)}, f32[512,1024]{1,0:T(8,128)}, u32[]{:S(2)}, u32[]{:S(2)}) collective-permute-start(f32[512,1024]{1,0:T(8,128)} %constant_dynamic-update-slice_fusion.2.mine_ref), channel_id=1, source_target_pairs={{0,1},{1,0},{2,3},{3,2},{4,5},{5,4},{6,7},{7,6},{8,9},{9,8},{10,11... | collective-permute-start | bytes 6291464 | tf_op jit(solution)/shard_map/ppermute | solution.py:419
  356.8 105.2 %collective-permute-start.27 = (f32[512,1024]{1,0:T(8,128)}, f32[512,1024]{1,0:T(8,128)}, u32[]{:S(2)}, u32[]{:S(2)}) collective-permute-start(f32[512,1024]{1,0:T(8,128)} %convolution_add_fusion), channel_id=1, source_target_pairs={{0,2},{1,3},{2,0},{3,1},{4,6},{5,7},{6,4},{7,5},{8,10},{9,11},{10,... | collective-permute-start | bytes 6291464 | tf_op jit(solution)/shard_map/ppermute | solution.py:422
  383.9 36.9 %collective-permute-start.28 = (f32[4,776,128]{2,1,0:T(8,128)}, f32[4,776,128]{2,1,0:T(8,128)S(1)}, u32[]{:S(2)}, u32[]{:S(2)}) collective-permute-start(f32[4,776,128]{2,1,0:T(8,128)} %get-tuple-element.187), channel_id=1, source_target_pairs={{0,4},{4,0},{8,12},{12,8},{16,20},{20,16},{24,28},{28,24},{1,5},{5... | collective-permute-start | bytes 4767752 | tf_op jit(solution)/shard_map/ppermute | solution.py:458
  420.0 43.6 %collective-permute-start.32 = (f32[3,8,128,128]{3,2,1,0:T(8,128)}, f32[3,8,128,128]{3,2,1,0:T(8,128)S(1)}, u32[]{:S(2)}, u32[]{:S(2)}) collective-permute-start(f32[3,8,128,128]{3,2,1,0:T(8,128)} %get-tuple-element.186), channel_id=1, source_target_pairs={{0,4},{4,0},{8,12},{12,8},{16,20},{20,16},{24,28},{28,24},{1,5},{5... | collective-permute-start | bytes 4718600 | tf_op jit(solution)/shard_map/ppermute | solution.py:458
  421.9 41.6 %collective-permute-start.31 = (f32[776,128]{1,0:T(8,128)}, f32[776,128]{1,0:T(8,128)S(1)}, u32[]{:S(2)}, u32[]{:S(2)}) collective-permute-start(f32[776,128]{1,0:T(8,128)} %get-tuple-element.255), channel_id=1, source_target_pairs={{0,24},{4,28},{8,0},{12,4},{16,8},{20,12},{24,16},{28,20},{1,25},{... | collective-permute-start | bytes 1191944 | tf_op jit(solution)/shard_map/ppermute | solution.py:440
  426.2 37.4 %collective-permute-start.30 = (f32[776,128]{1,0:T(8,128)S(1)}, f32[776,128]{1,0:T(8,128)S(1)}, u32[]{:S(2)}, u32[]{:S(2)}) collective-permute-start(f32[776,128]{1,0:T(8,128)S(1)} %get-tuple-element.256), channel_id=1, source_target_pairs={{0,16},{4,20},{8,24},{12,28},{16,0},{20,4},{24,8},{28,12},{1,17},{... | collective-permute-start | bytes 1191944 | tf_op jit(solution)/shard_map/ppermute | solution.py:440
  426.2 37.4 %collective-permute-start.29 = (f32[776,128]{1,0:T(8,128)S(1)}, f32[776,128]{1,0:T(8,128)S(1)}, u32[]{:S(2)}, u32[]{:S(2)}) collective-permute-start(f32[776,128]{1,0:T(8,128)S(1)} %get-tuple-element.257), channel_id=1, source_target_pairs={{0,8},{4,12},{8,16},{12,20},{16,24},{20,28},{24,0},{28,4},{1,9},{5... | collective-permute-start | bytes 1191944 | tf_op jit(solution)/shard_map/ppermute | solution.py:440
  462.0 45.4 %collective-permute-start.37 = (f32[3,10,128,128]{3,2,1,0:T(8,128)}, f32[3,10,128,128]{3,2,1,0:T(8,128)S(1)}, u32[]{:S(2)}, u32[]{:S(2)}) collective-permute-start(f32[3,10,128,128]{3,2,1,0:T(8,128)} %get-tuple-element.183), channel_id=1, source_target_pairs={{0,4},{4,0},{8,12},{12,8},{16,20},{20,16},{24,28},{28,24},{1,5},{5... | collective-permute-start | bytes 5898248 | tf_op jit(solution)/shard_map/ppermute | solution.py:458
  467.5 39.0 %collective-permute-start.35 = (f32[512,1024]{1,0:T(8,128)}, f32[512,1024]{1,0:T(8,128)S(1)}, u32[]{:S(2)}, u32[]{:S(2)}) collective-permute-start(f32[512,1024]{1,0:T(8,128)} %get-tuple-element.198), channel_id=1, source_target_pairs={{0,1},{1,0},{2,3},{3,2},{4,5},{5,4},{6,7},{7,6},{8,9},{9,8},{10,11... | collective-permute-start | bytes 6291464 | tf_op jit(solution)/shard_map/ppermute | solution.py:419
  472.8 35.3 %collective-permute-start.40 = (f32[2,128]{1,0:T(2,128)S(1)}, f32[2,128]{1,0:T(2,128)S(1)}, u32[]{:S(2)}, u32[]{:S(2)}) collective-permute-start(f32[2,128]{1,0:T(2,128)S(1)} %get-tuple-element.281), channel_id=1, source_target_pairs={{0,24},{4,28},{8,0},{12,4},{16,8},{20,12},{24,16},{28,20},{1,25},{... | collective-permute-start | bytes 3080 | tf_op jit(solution)/shard_map/ppermute | solution.py:440
  477.0 56.6 %collective-permute-start.38 = (f32[2,128]{1,0:T(2,128)S(1)}, f32[2,128]{1,0:T(2,128)S(1)}, u32[]{:S(2)}, u32[]{:S(2)}) collective-permute-start(f32[2,128]{1,0:T(2,128)S(1)} %get-tuple-element.283), channel_id=1, source_target_pairs={{0,8},{4,12},{8,16},{12,20},{16,24},{20,28},{24,0},{28,4},{1,9},{5... | collective-permute-start | bytes 3080 | tf_op jit(solution)/shard_map/ppermute | solution.py:440
  506.5 59.3 %collective-permute-start.44 = (f32[512,1024]{1,0:T(8,128)}, f32[512,1024]{1,0:T(8,128)}, u32[]{:S(2)}, u32[]{:S(2)}) collective-permute-start(f32[512,1024]{1,0:T(8,128)} %subtract_add_fusion.mine_ref), channel_id=1, source_target_pairs={{0,1},{1,0},{2,3},{3,2},{4,5},{5,4},{6,7},{7,6},{8,9},{9,8},{10,11... | collective-permute-start | bytes 6291464 | tf_op jit(solution)/shard_map/ppermute | solution.py:419
  507.5 37.1 %collective-permute-start.42 = (f32[3,8,128,128]{3,2,1,0:T(8,128)}, f32[3,8,128,128]{3,2,1,0:T(8,128)S(1)}, u32[]{:S(2)}, u32[]{:S(2)}) collective-permute-start(f32[3,8,128,128]{3,2,1,0:T(8,128)} %get-tuple-element.200), channel_id=1, source_target_pairs={{0,4},{4,0},{8,12},{12,8},{16,20},{20,16},{24,28},{28,24},{1,5},{5... | collective-permute-start | bytes 4718600 | tf_op jit(solution)/shard_map/ppermute | solution.py:458
  508.7 47.3 %collective-permute-start.41 = (f32[256,1024]{1,0:T(8,128)S(1)}, f32[256,1024]{1,0:T(8,128)}, u32[]{:S(2)}, u32[]{:S(2)}) collective-permute-start(f32[256,1024]{1,0:T(8,128)S(1)} %get-tuple-element.249), channel_id=1, source_target_pairs={{0,2},{1,3},{2,0},{3,1},{4,6},{5,7},{6,4},{7,5},{8,10},{9,11},{10,... | collective-permute-start | bytes 3145736 | tf_op jit(solution)/shard_map/ppermute | solution.py:422
  (113 other events, 1048.7 us)
